TPU v7x, 32 devices: a whole 2x2x4 slice. The times are simulated.
32 devices in a mesh: groups: 2 (over y), lat: 4 (over x, core), lon: 4 (over z).
Axes of the slice: x: 2, y: 2, z: 4, core: 2. Of those that a mesh axis runs over, the one named last changes fastest.
Arguments:
- fields: bfloat16 [512, 4, 512], P('groups', 'lat', 'lon'), parts along dimension 0, may hold values from -6 to 6
- upstream: bfloat16 [512, 4, 512], P('groups', 'lat', 'lon'), parts along dimension 0, may hold values from -6 to 6
- weights: bfloat16 [9, 256, 256], replicated, may hold values from -0.125 to 0.125
- filter_taps: bfloat16 [4, 9, 3, 2, 64], P('lat'), may hold values from -0.3125 to 0.3125
- cycle_counts: int32 [4], P('lat'), may hold values from 1 to 2, as said below
- cycle_blocks: int32 [4, 2], P('lat'), may hold values from -2 to 1, as said below
Outputs:
- outputs: bfloat16 [512, 4, 512], P('groups', 'lat', 'lon'), parts along dimension 0
- input_grad: bfloat16 [512, 4, 512], P('groups', 'lat', 'lon'), parts along dimension 0
- weight_grad: float32 [18, 256, 256], P('groups', 'lon'), parts along dimension 0
There are 2 independent parts, one for each index of `groups`. A program takes and returns all parts, laid end to end along the dimension named above; an argument that names none is the same for every part. Nothing has to cross between parts.
Inputs may be any that keep to these rules, and one draw needn't show every extreme that they name: Cycle i uses its first cycle_counts[i] slots; the first quarter of the cycles (at least one) uses all 2, the last cycle one. `cycle_blocks`: the 2 block numbers of a cycle are distinct; the first cycle holds the lowest and the highest.
All inputs are finite; a program needn't handle non-finite values.
Results may differ from a plain program's by a relative error of at most 0.0049.
Values may be sent and summed in bfloat16 or wider, within the bound.
A program may use at most 64 MiB of HBM per device.

v0:
```python
import jax
import jax.numpy as jnp
from jax import lax
from jax.sharding import PartitionSpec as P

HALO = 128


def padded_2(cells, sides, width, closed):
    for axis, dim in sides:
        count = lax.axis_size(axis)
        ends = count if closed else count - 1
        head = lax.slice_in_dim(cells, 0, width, axis=dim)
        tail = lax.slice_in_dim(cells, cells.shape[dim] - width, cells.shape[dim], axis=dim)
        cells = jnp.concatenate(
            [
                lax.ppermute(tail, axis, [(i, (i + 1) % count) for i in range(ends)]),
                cells,
                lax.ppermute(head, axis, [((i + 1) % count, i) for i in range(ends)]),
            ],
            axis=dim,
        )
    return cells


def build_taps(filter_taps, cycle_counts, cycle_blocks):
    slot_total = cycle_blocks.shape[1]
    width_block = filter_taps.shape[4]
    offsets = jnp.arange(width_block, dtype=jnp.int32)
    places = HALO + width_block * cycle_blocks[:, :, None] + offsets[None, None, :]
    live_slots = jnp.arange(slot_total, dtype=jnp.int32)[None, :] < cycle_counts[:, None]
    positions = jnp.arange(2 * HALO, dtype=jnp.int32)
    onehot = jnp.where(
        (places[:, :, :, None] == positions) & live_slots[:, :, None, None], 1.0, 0.0
    ).astype(jnp.float32)
    return jnp.einsum("ikrst,istu->ikru", filter_taps.astype(jnp.float32), onehot)


def banded_matrix(tap_row, out_width, tap_reach):
    kernels = tap_row.shape[0]
    stencil_rows = tap_row.shape[1]
    window_len = out_width + tap_reach
    padded = jnp.concatenate(
        [tap_row, jnp.zeros((kernels, stencil_rows, window_len + 1 - tap_reach), tap_row.dtype)],
        axis=2,
    )
    repeated = jnp.tile(padded, (1, 1, out_width))[:, :, : out_width * window_len]
    repeated = repeated.reshape(kernels, stencil_rows, out_width, window_len)
    return jnp.transpose(repeated, (1, 3, 0, 2))


def body(fields, upstream, weights, filter_taps, cycle_counts, cycle_blocks):
    channels, lat_rows, lon_cols = fields.shape
    kernels = weights.shape[0]
    window_len = lon_cols + 2 * HALO
    tap_table = build_taps(filter_taps, cycle_counts, cycle_blocks).astype(jnp.bfloat16)
    banded = padded_2(fields, (("lat", 1),), 1, False)
    widened = padded_2(banded, (("lon", 2),), HALO, True)
    matrices = [
        banded_matrix(tap_table[0], lon_cols, 2 * HALO).reshape(3 * window_len, kernels * lon_cols)
    ]
    cycle_row = 0
    responses = [
        jnp.dot(
            widened.reshape(channels, 3 * window_len),
            matrices[cycle_row],
            preferred_element_type=jnp.float32,
        )
    ]
    response = (
        jnp.stack(responses, axis=1)
        .reshape(channels, lat_rows, kernels, lon_cols)
        .astype(jnp.bfloat16)
    )
    outputs = jnp.einsum(
        "koc,cikj->oij", weights, response, preferred_element_type=jnp.float32
    ).astype(jnp.bfloat16)
    response_grad = jnp.einsum(
        "koc,oij->cikj", weights, upstream, preferred_element_type=jnp.float32
    ).astype(jnp.bfloat16)
    grad_terms = jnp.einsum("oij,cikj->koc", upstream, response, preferred_element_type=jnp.float32)
    grad_share = lax.psum_scatter(grad_terms, "lon", scatter_dimension=1, tiled=True)
    weight_grad = lax.psum(grad_share, "lat")
    accumulated = jnp.zeros((channels, lat_rows + 2, window_len), jnp.float32)
    cycle_row = 0
    grad_piece = response_grad[:, cycle_row].reshape(channels, kernels * lon_cols)
    contrib = jnp.einsum(
        "cn,mn->cm", grad_piece, matrices[cycle_row], preferred_element_type=jnp.float32
    )
    accumulated = accumulated.at[:, cycle_row : cycle_row + 3].add(
        contrib.reshape(channels, 3, window_len)
    )
    rim_columns = jnp.concatenate(
        [accumulated[:, :, :HALO], accumulated[:, :, HALO + lon_cols :]], axis=2
    )
    arrived = padded_2(rim_columns, (("lon", 2),), HALO, True)
    interior = accumulated[:, :, HALO : HALO + lon_cols]
    interior = interior.at[:, :, :HALO].add(arrived[:, :, :HALO])
    interior = interior.at[:, :, lon_cols - HALO :].add(arrived[:, :, 3 * HALO :])
    edge_rows = jnp.stack([interior[:, 0], interior[:, lat_rows + 1]], axis=1)
    arrived = padded_2(edge_rows, (("lat", 1),), 1, False)
    result = interior[:, 1 : lat_rows + 1]
    result = result.at[:, 0].add(arrived[:, 0])
    result = result.at[:, lat_rows - 1].add(arrived[:, 3])
    return (outputs, result.astype(jnp.bfloat16), weight_grad)


def solution(mesh):
    return jax.shard_map(
        body,
        mesh=mesh,
        in_specs=(
            P("groups", "lat", "lon"),
            P("groups", "lat", "lon"),
            P(),
            P("lat", None, None, None, None),
            P("lat"),
            P("lat", None),
        ),
        out_specs=(P("groups", "lat", "lon"), P("groups", "lat", "lon"), P("groups", "lon", None)),
        check_vma=False,
    )
```

profile of v0, /device:TPU:1, one launch (start us, length us, event | category | flops | bytes accessed | tf_op | source)
XLA Modules:
  0.0 197.0 jit_solution(18379826614206599920)
XLA Ops:
  7.2 1.0 copy.32
  8.3 2.0 collective-permute-start.1
  10.2 4.5 %collective-permute-start = (bf16[256,1,128]{0,2,1:T(8,128)(2,1)S(1)}, bf16[256,1,128]{0,2,1:T(8,128)(2,1)S(1)}, u32[]{:S(2)}, u32[]{:S(2)}) collective-permute-start(bf16[256,1,128]{0,2,1:T(8,128)(2,1)S(1)} %copy.32), channel_id=1, source_target_pairs={{0,4},{4,8},{8,12},{1,5},{5,9},{9,13},{2,6},{6,10},{10,14},{3,7},{... | collective-permute-start | bytes 196616 | tf_op jit(solution)/shard_map/ppermute | solution.py:17
  16.1 3.4 %collective-permute-start.3 = (bf16[256,3,128]{0,2,1:T(8,128)(2,1)S(1)}, bf16[256,3,128]{0,2,1:T(8,128)(2,1)S(1)}, u32[]{:S(2)}, u32[]{:S(2)}) collective-permute-start(bf16[256,3,128]{0,2,1:T(8,128)(2,1)S(1)} %pad_maximum_fusion.1), channel_id=1, source_target_pairs={{1,0},{2,1},{3,2},{0,3},{5,4},{6,5},{7,6},{4,7},{9,8},{10,9},{11,1... | collective-permute-start | bytes 589832 | tf_op jit(solution)/shard_map/ppermute | solution.py:19
  19.5 0.9 fusion.3
  20.5 2.1 %tile.4 = bf16[9,3,128,385]{3,2,1,0:T(8,128)(2,1)} broadcast(bf16[9,3,385]{2,1,0:T(4,128)(2,1)S(1)} %concatenate.21.clone), dimensions={0,1,3} | broadcast | bytes 2681910 | tf_op jit(solution)/shard_map/tile | solution.py:47
  22.5 11.0 %tile.10 = bf16[9,3,49280]{2,1,0:T(4,128)(2,1)} reshape(bf16[9,3,128,385]{3,2,1,0:T(8,128)(2,1)} %tile.4) | data formatting | bytes 5322240 | tf_op jit(solution)/shard_map/tile | solution.py:47
  33.6 5.1 %slice.123 = bf16[9,3,49152]{2,1,0:T(4,128)(2,1)} slice(bf16[9,3,49280]{2,1,0:T(4,128)(2,1)} %tile.10), slice={[0:9], [0:3], [0:49152]} | slice | bytes 5308416 | tf_op jit(solution)/shard_map/slice | solution.py:47
  38.7 8.2 %reshape.267 = bf16[9,3,128,384]{3,2,1,0:T(8,128)(2,1)} reshape(bf16[9,3,49152]{2,1,0:T(4,128)(2,1)} %slice.123) | data formatting | bytes 5308416 | tf_op jit(solution)/shard_map/reshape | solution.py:48
  46.9 4.0 %copy.37 = bf16[3,384,9,128]{1,0,3,2:T(4,128)(2,1)S(1)} copy(bf16[3,384,9,128]{1,3,0,2:T(8,128)(2,1)} %bitcast.68) | data formatting | bytes 5308416 | tf_op jit(solution)/shard_map/transpose | solution.py:49
  51.5 1.1 convolution_convert_fusion.1
  52.7 0.8 copy-done.1
  53.9 3.4 %copy.44 = f32[9,256,256]{2,0,1:T(8,128)} copy(f32[9,256,256]{1,2,0:T(8,128)S(1)} %convolution_bitcast_fusion) | data formatting | bytes 4718592 | tf_op jit(solution)/shard_map/oij,cikj->koc/transpose | solution.py:81
  57.4 2.0 %copy.41 = bf16[3,384,9,128]{1,3,2,0:T(8,128)(2,1)S(1)} copy(bf16[3,384,9,128]{1,3,0,2:T(8,128)(2,1)} %bitcast.69) | data formatting | bytes 5308416 | tf_op jit(solution)/shard_map/transpose | solution.py:49
  59.9 1.0 fusion.22
  61.0 3.3 %collective-permute-start.5 = (f32[256,3,128]{2,0,1:T(8,128)S(1)}, f32[256,3,128]{2,0,1:T(8,128)S(1)}, u32[]{:S(2)}, u32[]{:S(2)}) collective-permute-start(f32[256,3,128]{2,0,1:T(8,128)S(1)} %get-tuple-element.97), channel_id=1, source_target_pairs={{1,0},{2,1},{3,2},{0,3},{5,4},{6,5},{7,6},{4,7},{9,8},{10,9},{11,1... | collective-permute-start | bytes 1179656 | tf_op jit(solution)/shard_map/ppermute | solution.py:19
  64.3 13.4 %collective-permute-done.4 = f32[256,3,128]{2,0,1:T(8,128)S(1)} collective-permute-done((f32[256,3,128]{2,0,1:T(8,128)S(1)}, f32[256,3,128]{2,0,1:T(8,128)S(1)}, u32[]{:S(2)}, u32[]{:S(2)}) %collective-permute-start.4) | collective-permute-done | bytes 393248 | tf_op jit(solution)/shard_map/ppermute | solution.py:17
  77.7 14.8 %collective-permute-done.5 = f32[256,3,128]{2,0,1:T(8,128)S(1)} collective-permute-done((f32[256,3,128]{2,0,1:T(8,128)S(1)}, f32[256,3,128]{2,0,1:T(8,128)S(1)}, u32[]{:S(2)}, u32[]{:S(2)}) %collective-permute-start.5) | collective-permute-done | bytes 393248 | tf_op jit(solution)/shard_map/ppermute | solution.py:19
  92.6 7.2 %collective-permute-start.6 = (f32[256,1,128]{2,0,1:T(8,128)S(1)}, f32[256,1,128]{2,0,1:T(8,128)S(1)}, u32[]{:S(2)}, u32[]{:S(2)}) collective-permute-start(f32[256,1,128]{2,0,1:T(8,128)S(1)} %get-tuple-element.98), channel_id=1, source_target_pairs={{0,4},{4,8},{8,12},{1,5},{5,9},{9,13},{2,6},{6,10},{10,14},{3,7},{... | collective-permute-start | bytes 393224 | tf_op jit(solution)/shard_map/ppermute | solution.py:17
  99.8 1.9 collective-permute-start.7
  101.8 47.6 %reduce-scatter.2.cloned.1.call-done = f32[9,64,256]{2,0,1:T(8,128)} async-done(((f32[9,256,256]{2,0,1:T(8,128)}), f32[9,64,256]{2,0,1:T(8,128)}) %reduce-scatter.2.cloned.1.call-update) | async-done | bytes 589840 | tf_op jit(solution)/shard_map/reduce_scatter | solution.py:82
  150.0 0.7 copy.45
  151.4 36.4 %all-reduce.3.cloned.1.call-done = f32[9,64,256]{2,0,1:T(8,128)} async-done(((f32[9,64,256]{2,0,1:T(8,128)}), f32[9,64,256]{2,0,1:T(8,128)}) %all-reduce.3.cloned.1.call-update) | async-done | bytes 589840 | tf_op jit(solution)/shard_map/psum | solution.py:83
  187.8 2.4 %copy.46 = f32[9,64,256]{2,1,0:T(8,128)} copy(f32[9,64,256]{2,0,1:T(8,128)} %all-reduce.3.cloned.1.call-done) | data formatting | bytes 1179648
  (36 shorter events, 3.7 us)
Async XLA Ops:
  7.2 52.3 %copy-start = (bf16[9,256,256]{2,1,0:T(8,128)(2,1)S(1)}, bf16[9,256,256]{2,1,0:T(8,128)(2,1)}, u32[]{:S(2)}) copy-start(bf16[9,256,256]{2,1,0:T(8,128)(2,1)} %param.24) | copy-start | bytes 3538948
  7.2 142.2 %reduce-scatter.2.cloned.1.call-start = ((), (), s32[]{:S(2)}) async-start(), calls=%async_computation.1 | async-start | bytes 5242880 | tf_op jit(solution)/shard_map/reduce_scatter | solution.py:82
  8.3 7.8 %collective-permute-start.1 = (bf16[256,1,128]{0,2,1:T(8,128)(2,1)S(1)}, bf16[256,1,128]{0,2,1:T(8,128)(2,1)S(1)}, u32[]{:S(2)}, u32[]{:S(2)}) collective-permute-start(bf16[256,1,128]{0,2,1:T(8,128)(2,1)S(1)} %copy.32), channel_id=1, source_target_pairs={{4,0},{8,4},{12,8},{5,1},{9,5},{13,9},{6,2},{10,6},{14,10},{7,3},{... | collective-permute-start | bytes 196616 | tf_op jit(solution)/shard_map/ppermute | solution.py:19
  10.2 5.9 %collective-permute-start = (bf16[256,1,128]{0,2,1:T(8,128)(2,1)S(1)}, bf16[256,1,128]{0,2,1:T(8,128)(2,1)S(1)}, u32[]{:S(2)}, u32[]{:S(2)}) collective-permute-start(bf16[256,1,128]{0,2,1:T(8,128)(2,1)S(1)} %copy.32), channel_id=1, source_target_pairs={{0,4},{4,8},{8,12},{1,5},{5,9},{9,13},{2,6},{6,10},{10,14},{3,7},{... | collective-permute-start | bytes 196616 | tf_op jit(solution)/shard_map/ppermute | solution.py:17
  16.1 35.3 %collective-permute-start.3 = (bf16[256,3,128]{0,2,1:T(8,128)(2,1)S(1)}, bf16[256,3,128]{0,2,1:T(8,128)(2,1)S(1)}, u32[]{:S(2)}, u32[]{:S(2)}) collective-permute-start(bf16[256,3,128]{0,2,1:T(8,128)(2,1)S(1)} %pad_maximum_fusion.1), channel_id=1, source_target_pairs={{1,0},{2,1},{3,2},{0,3},{5,4},{6,5},{7,6},{4,7},{9,8},{10,9},{11,1... | collective-permute-start | bytes 589832 | tf_op jit(solution)/shard_map/ppermute | solution.py:19
  19.5 32.0 %collective-permute-start.2 = (bf16[256,3,128]{0,2,1:T(8,128)(2,1)S(1)}, bf16[256,3,128]{0,2,1:T(8,128)(2,1)S(1)}, u32[]{:S(2)}, u32[]{:S(2)}) collective-permute-start(bf16[256,3,128]{0,2,1:T(8,128)(2,1)S(1)} %pad_maximum_fusion.1), channel_id=1, source_target_pairs={{0,1},{1,2},{2,3},{3,0},{4,5},{5,6},{6,7},{7,4},{8,9},{9,10},{10,1... | collective-permute-start | bytes 589832 | tf_op jit(solution)/shard_map/ppermute | solution.py:17
  51.5 1.9 copy-start.3
  52.6 0.8 copy-start.1
  57.4 2.1 %copy-start.4 = (bf16[256,1,128]{2,0,1:T(8,128)(2,1)S(1)}, bf16[256,1,128]{2,0,1:T(8,128)(2,1)}, u32[]{:S(2)}) copy-start(bf16[256,1,128]{2,0,1:T(8,128)(2,1)} %param.23) | copy-start | bytes 196612
  57.4 130.4 %all-reduce.3.cloned.1.call-start = ((), (), s32[]{:S(2)}) async-start(), calls=%async_computation.2 | async-start | bytes 2097152 | tf_op jit(solution)/shard_map/psum | solution.py:83
  61.0 16.7 %collective-permute-start.4 = (f32[256,3,128]{2,0,1:T(8,128)S(1)}, f32[256,3,128]{2,0,1:T(8,128)S(1)}, u32[]{:S(2)}, u32[]{:S(2)}) collective-permute-start(f32[256,3,128]{2,0,1:T(8,128)S(1)} %get-tuple-element.96), channel_id=1, source_target_pairs={{0,1},{1,2},{2,3},{3,0},{4,5},{5,6},{6,7},{7,4},{8,9},{9,10},{10,1... | collective-permute-start | bytes 1179656 | tf_op jit(solution)/shard_map/ppermute | solution.py:17
  61.0 31.5 %collective-permute-start.5 = (f32[256,3,128]{2,0,1:T(8,128)S(1)}, f32[256,3,128]{2,0,1:T(8,128)S(1)}, u32[]{:S(2)}, u32[]{:S(2)}) collective-permute-start(f32[256,3,128]{2,0,1:T(8,128)S(1)} %get-tuple-element.97), channel_id=1, source_target_pairs={{1,0},{2,1},{3,2},{0,3},{5,4},{6,5},{7,6},{4,7},{9,8},{10,9},{11,1... | collective-permute-start | bytes 1179656 | tf_op jit(solution)/shard_map/ppermute | solution.py:19
  92.6 56.9 %copy-start.2 = (bf16[256,9,128]{2,0,1:T(8,128)(2,1)S(1)}, bf16[256,9,128]{2,0,1:T(8,128)(2,1)}, u32[]{:S(2)}) copy-start(bf16[256,9,128]{2,0,1:T(8,128)(2,1)} %copy-done.1) | copy-start | bytes 1769476
  92.6 58.1 %collective-permute-start.6 = (f32[256,1,128]{2,0,1:T(8,128)S(1)}, f32[256,1,128]{2,0,1:T(8,128)S(1)}, u32[]{:S(2)}, u32[]{:S(2)}) collective-permute-start(f32[256,1,128]{2,0,1:T(8,128)S(1)} %get-tuple-element.98), channel_id=1, source_target_pairs={{0,4},{4,8},{8,12},{1,5},{5,9},{9,13},{2,6},{6,10},{10,14},{3,7},{... | collective-permute-start | bytes 393224 | tf_op jit(solution)/shard_map/ppermute | solution.py:17
  99.8 50.9 %collective-permute-start.7 = (f32[256,1,128]{2,0,1:T(8,128)S(1)}, f32[256,1,128]{2,0,1:T(8,128)S(1)}, u32[]{:S(2)}, u32[]{:S(2)}) collective-permute-start(f32[256,1,128]{2,0,1:T(8,128)S(1)} %get-tuple-element.99), channel_id=1, source_target_pairs={{4,0},{8,4},{12,8},{5,1},{9,5},{13,9},{6,2},{10,6},{14,10},{7,3},{... | collective-permute-start | bytes 393224 | tf_op jit(solution)/shard_map/ppermute | solution.py:19
Sparse Core Ops, SparseCore 0:
  57.5 91.8 reduce-scatter.1
  151.9 35.8 all-reduce.2
where the time goes:
time: 199 us; the launch traced here: 197 us
  waiting for transfers between devices  112 us (56%)
  local copies, waits for them, and re-layouts  41.5 us (21%)
  starting transfers between devices  22.4 us (11%)
  between operations  14.9 us (7%)
  matrix products  4.4 us (2%)
    reduce_scatter x1, waiting for transfers between devices, body(): lax.psum_scatter(grad_terms, 'lon', scatter_dimension=1, tiled=True)  47.6 us
    psum x1, waiting for transfers between devices, body(): weight_grad = lax.psum(grad_share, 'lat')  36.4 us
    ppermute x4, waiting for transfers between devices, padded_2(): lax.ppermute(head, axis, [((i + 1) % count, i) for i in range(ends)])  14.8 us
    ppermute x4, waiting for transfers between devices, padded_2(): lax.ppermute(tail, axis, [(i, (i + 1) % count) for i in range(ends)])  13.4 us
    another operation x2, local copies, waits for them, and re-layouts, banded_matrix(): jnp.tile(padded, (1, 1, out_width))[:, :, :out_width * window_len]  13.1 us
    ppermute x4, starting transfers between devices, padded_2(): lax.ppermute(tail, axis, [(i, (i + 1) % count) for i in range(ends)])  11.8 us
    ppermute x4, starting transfers between devices, padded_2(): lax.ppermute(head, axis, [((i + 1) % count, i) for i in range(ends)])  10.6 us
    reshape x1, local copies, waits for them, and re-layouts, banded_matrix(): repeated = repeated.reshape(kernels, stencil_rows, out_width, window_len)  8.24 us
  transfers between devices with their start and end apart: 10, of which 4 were waited for; matrix products, arithmetic and copies ran while one was open for 19% of the time, Pallas kernels for 0%

commit v1 on v0

v1 whole, which is shorter than its diff:
```python
import functools

import jax
import jax.numpy as jnp
from jax import lax
from jax.experimental import pallas as pl
from jax.experimental.pallas import tpu as pltpu
from jax.sharding import PartitionSpec as P

HALO = 128
MESH = pl.DeviceIdType.MESH
NT = (((1,), (1,)), ((), ()))
TN = (((0,), (0,)), ((), ()))


def tap_rows(filter_taps, cycle_counts, cycle_blocks):
    kernels, stencil, slots, width = filter_taps.shape[1:]
    taps = filter_taps[0].astype(jnp.float32)
    live = jnp.arange(slots, dtype=jnp.int32) < cycle_counts[0]
    pieces = []
    for block in range(2 * HALO // width):
        here = live & (cycle_blocks[0] + HALO // width == block)
        pieces.append(jnp.sum(jnp.where(here[None, None, :, None], taps, 0.0), axis=2))
    table = jnp.concatenate(pieces, axis=2).reshape(kernels * stencil, 2 * HALO)
    return jnp.pad(table, ((0, 0), (0, 2 * HALO)))


def kernel(
    n_lat, n_lon, taps_ref, f_ref, u_ref, w_ref, out_ref, grad_ref, wg_ref,
    f_all, u_all, u_chunk, band, resp, rg, g_mine, g_got,
    part, part_got, chip, result,
    zf_s, zf_r, zu_s, zu_r, lf_s, lf_r, g_s, g_r, p_s, p_r, x_s, x_r, q_s, q_r,
):
    kernels, channels, _ = w_ref.shape
    width = f_ref.shape[1]
    chunk = u_chunk.shape[1]
    chips = n_lat // 2
    a = lax.axis_index("lat")
    b = lax.axis_index("lon")
    core = lax.rem(a, 2)
    chip_at = a // 2
    twin = a + 1 - 2 * core
    has_up = a < n_lat - 1
    has_down = a > 0

    def lon_peer(step):
        return {"lat": a, "lon": lax.rem(b + step, n_lon)}

    def lat_peer(at):
        return {"lat": at, "lon": b}

    barrier = pltpu.get_barrier_semaphore()
    for step in range(1, n_lon):
        pl.semaphore_signal(barrier, inc=1, device_id=lon_peer(step), device_id_type=MESH)
    for step in range(1, n_lat):
        pl.semaphore_signal(
            barrier, inc=1, device_id=lat_peer(lax.rem(a + step, n_lat)), device_id_type=MESH
        )
    pl.semaphore_wait(barrier, n_lon + n_lat - 2)

    def remote(src, dst, send, recv, to):
        return pltpu.make_async_remote_copy(
            src_ref=src, dst_ref=dst, send_sem=send, recv_sem=recv, device_id=to,
            device_id_type=MESH,
        )

    def send_f(step):
        slot = n_lon - step
        return remote(f_ref, f_all.at[1, slot], zf_s.at[step], zf_r.at[slot], lon_peer(step))

    def send_u(step):
        slot = n_lon - step
        if step in (1, n_lon - 1):
            return remote(u_ref, u_all.at[slot], zu_s.at[step], zu_r.at[slot], lon_peer(step))
        start = pl.multiple_of(lax.rem(b + step, n_lon) * chunk, chunk)
        return remote(
            u_ref.at[pl.ds(start, chunk)], u_chunk.at[slot], zu_s.at[step], zu_r.at[slot],
            lon_peer(step),
        )

    def lat_f(way, slot):
        to = a + 1 if way == 0 else a - 1
        src = f_ref if slot == 0 else f_all.at[1, slot]
        return remote(
            src, f_all.at[2 * way, slot], lf_s.at[way, slot], lf_r.at[way, slot], lat_peer(to)
        )

    steps = sorted(range(1, n_lon), key=lambda step: min(step, n_lon - step), reverse=True)
    for step in steps:
        send_f(step).start()

    @pl.when(has_up)
    def _():
        lat_f(0, 0).start()

    @pl.when(has_down)
    def _():
        lat_f(1, 0).start()

    for step in steps:
        send_u(step).start()

    for k in range(kernels):
        for r in range(3):
            row = taps_ref[3 * k + r : 3 * k + r + 1, :]
            turned = pltpu.roll(
                jnp.broadcast_to(row, (width, 4 * HALO)), 0, 1, stride=1, stride_axis=0
            ).astype(jnp.bfloat16)
            for d in range(3):
                band[k * width : (k + 1) * width, (3 * d + r) * width : (3 * d + r + 1) * width] = (
                    turned[:, d * width : (d + 1) * width]
                )

    f_all[1, 0] = f_ref[...]
    u_all[0] = u_ref[...]

    @pl.when(jnp.logical_not(has_down))
    def _():
        f_all[0] = jnp.zeros(f_all.shape[1:], f_all.dtype)

    @pl.when(jnp.logical_not(has_up))
    def _():
        f_all[2] = jnp.zeros(f_all.shape[1:], f_all.dtype)

    for step in steps[::-1]:
        slot = n_lon - step
        send_f(step).wait_recv()

        @pl.when(has_up)
        def _():
            lat_f(0, slot).start()

        @pl.when(has_down)
        def _():
            lat_f(1, slot).start()

    for step in (1, n_lon - 1):
        send_u(step).wait_recv()
    u_wide = jnp.concatenate([u_all[n_lon - 1], u_all[0], u_all[1]], axis=1)
    for k in range(kernels):
        mixed = lax.dot_general(
            w_ref[k], u_wide, TN, preferred_element_type=jnp.float32
        ).astype(jnp.bfloat16)
        for j in range(3):
            rg[j, :, k * width : (k + 1) * width] = mixed[:, j * width : (j + 1) * width]
    terms = jnp.zeros((channels, 3 * width), jnp.float32)
    for j in range(3):
        terms = terms + jnp.dot(
            rg[j], band[:, (2 - j) * 3 * width : (3 - j) * 3 * width],
            preferred_element_type=jnp.float32,
        )
    for r in range(3):
        g_mine[r] = terms[:, r * width : (r + 1) * width]

    def send_g(way):
        to = a + 1 if way == 0 else a - 1
        return remote(g_mine.at[2 - 2 * way], g_got.at[way], g_s.at[way], g_r.at[way], lat_peer(to))

    @pl.when(has_up)
    def _():
        send_g(0).start()

    @pl.when(has_down)
    def _():
        send_g(1).start()

    for slot in range(n_lon):
        @pl.when(has_down)
        def _():
            lat_f(0, slot).wait_recv()

        @pl.when(has_up)
        def _():
            lat_f(1, slot).wait_recv()

    group = 3 if kernels % 3 == 0 else 1

    @pl.loop(0, n_lon)
    def _(slot):
        window = jnp.concatenate(
            [f_all[r, lax.rem(slot + n_lon - 1 + d, n_lon)] for d in range(3) for r in range(3)],
            axis=1,
        )
        for k0 in range(0, kernels, group):
            got = lax.dot_general(
                window, band[k0 * width : (k0 + group) * width, :], NT,
                preferred_element_type=jnp.float32,
            ).astype(jnp.bfloat16)
            for k in range(group):
                resp[k0 + k, slot] = got[:, k * width : (k + 1) * width]

    rows = pl.ds(pl.multiple_of(b * chunk, chunk), chunk)
    for step in range(2, n_lon - 1):
        send_u(step).wait_recv()
    for slot in (0, 1, n_lon - 1):
        u_chunk[slot] = u_all[slot, rows, :]
    u_line = jnp.concatenate([u_chunk[slot] for slot in range(n_lon)], axis=1)
    for k in range(kernels):
        line = jnp.concatenate([resp[k, slot] for slot in range(n_lon)], axis=1)
        piece = lax.dot_general(u_line, line, NT, preferred_element_type=jnp.float32)
        for half in range(2):
            part[half, k * chunk : (k + 1) * chunk, :] = piece[
                :, half * channels // 2 : (half + 1) * channels // 2
            ]

    send_p = remote(part.at[1 - core], part_got, p_s, p_r, lat_peer(twin))
    send_p.start()

    def mix_out():
        total = jnp.zeros((channels, width), jnp.float32)
        for k in range(kernels):
            total = total + jnp.dot(w_ref[k], resp[k, 0], preferred_element_type=jnp.float32)
        out_ref[...] = total.astype(out_ref.dtype)

    send_p.wait_recv()
    chip[chip_at] = (part[core] + part_got[...]).astype(chip.dtype)

    def send_x(step):
        to = lax.rem(a + 2 * step, n_lat)
        return remote(
            chip.at[chip_at], chip.at[chip_at], x_s.at[step], x_r.at[chips - step], lat_peer(to)
        )

    def got_x(step):
        at = lax.rem(chip_at + chips - step, chips)
        return remote(
            chip.at[at], chip.at[at], x_s.at[step], x_r.at[chips - step], lat_peer(twin)
        )

    for step in range(1, chips):
        send_x(step).start()

    mix_out()

    @pl.when(has_down)
    def _():
        send_g(0).wait_recv()

    @pl.when(has_up)
    def _():
        send_g(1).wait_recv()

    below = jnp.where(has_down, g_got[0], 0.0)
    above = jnp.where(has_up, g_got[1], 0.0)
    grad_ref[...] = (g_mine[1] + below + above).astype(grad_ref.dtype)

    for step in range(1, chips):
        got_x(step).wait_recv()
    total = chip[0].astype(jnp.float32)
    for at in range(1, chips):
        total = total + chip[at].astype(jnp.float32)
    result[core] = total
    send_q = remote(result.at[core], result.at[core], q_s, q_r, lat_peer(twin))
    send_q.start()
    remote(result.at[1 - core], result.at[1 - core], q_s, q_r, lat_peer(twin)).wait_recv()
    wg_ref[:, : channels // 2] = result[0]
    wg_ref[:, channels // 2 :] = result[1]

    for step in range(1, n_lon):
        send_f(step).wait_send()
        send_u(step).wait_send()
    for slot in range(n_lon):
        @pl.when(has_up)
        def _():
            lat_f(0, slot).wait_send()

        @pl.when(has_down)
        def _():
            lat_f(1, slot).wait_send()

    @pl.when(has_up)
    def _():
        send_g(0).wait_send()

    @pl.when(has_down)
    def _():
        send_g(1).wait_send()

    send_p.wait_send()
    for step in range(1, chips):
        send_x(step).wait_send()
    send_q.wait_send()


def body(fields, upstream, weights, filter_taps, cycle_counts, cycle_blocks):
    channels, _, width = fields.shape
    kernels = weights.shape[0]
    n_lat, n_lon = lax.axis_size("lat"), lax.axis_size("lon")
    chunk = channels // n_lon
    taps = tap_rows(filter_taps, cycle_counts, cycle_blocks)
    bf16, f32 = jnp.bfloat16, jnp.float32
    dma = pltpu.SemaphoreType.DMA
    outputs, grad, weight_grad = pl.pallas_call(
        functools.partial(kernel, n_lat, n_lon),
        out_shape=(
            jax.ShapeDtypeStruct((channels, width), bf16),
            jax.ShapeDtypeStruct((channels, width), bf16),
            jax.ShapeDtypeStruct((kernels * chunk, channels), f32),
        ),
        in_specs=[pl.BlockSpec(memory_space=pltpu.VMEM)] * 4,
        out_specs=[pl.BlockSpec(memory_space=pltpu.VMEM)] * 3,
        scratch_shapes=[
            pltpu.VMEM((3, n_lon, channels, width), bf16),
            pltpu.VMEM((n_lon, channels, width), bf16),
            pltpu.VMEM((n_lon, chunk, width), bf16),
            pltpu.VMEM((kernels * width, 9 * width), bf16),
            pltpu.VMEM((kernels, n_lon, channels, width), bf16),
            pltpu.VMEM((3, channels, kernels * width), bf16),
            pltpu.VMEM((3, channels, width), f32),
            pltpu.VMEM((2, channels, width), f32),
            pltpu.VMEM((2, kernels * chunk, channels // 2), f32),
            pltpu.VMEM((kernels * chunk, channels // 2), f32),
            pltpu.VMEM((n_lat // 2, kernels * chunk, channels // 2), bf16),
            pltpu.VMEM((2, kernels * chunk, channels // 2), f32),
            dma((n_lon,)), dma((n_lon,)), dma((n_lon,)), dma((n_lon,)),
            dma((2, n_lon)), dma((2, n_lon)), dma((2,)), dma((2,)),
            dma, dma, dma((n_lat // 2,)), dma((n_lat // 2 + 1,)), dma, dma,
        ],
        compiler_params=pltpu.CompilerParams(
            collective_id=0, has_side_effects=True, vmem_limit_bytes=56 * 1024 * 1024
        ),
        cost_estimate=pl.CostEstimate(
            flops=8_000_000_000, bytes_accessed=3_000_000, transcendentals=0
        ),
    )(taps, fields.reshape(channels, width), upstream.reshape(channels, width), weights)
    return (
        outputs.reshape(fields.shape),
        grad.reshape(fields.shape),
        weight_grad.reshape(kernels, chunk, channels),
    )


def solution(mesh):
    return jax.shard_map(
        body,
        mesh=mesh,
        in_specs=(
            P("groups", "lat", "lon"),
            P("groups", "lat", "lon"),
            P(),
            P("lat", None, None, None, None),
            P("lat"),
            P("lat", None),
        ),
        out_specs=(P("groups", "lat", "lon"), P("groups", "lat", "lon"), P("groups", "lon", None)),
        check_vma=False,
    )
```

time: 199 us -> 40.3 us (0.20)
  the two profiles are of different devices: /device:TPU:1 before, /device:TPU:11 now
where the time goes in v1:
time: 40.3 us; the launch traced here: 39.9 us
  Pallas kernels  31.4 us (78%)
  local copies, waits for them, and re-layouts  5.51 us (14%)
  other arithmetic  1.71 us (4%)
  between operations  1.3 us (3%)
    pallas_call x1, Pallas kernels, body(): pl.pallas_call(functools.partial(kernel, n_lat, n_lon), out_shape=(jax.Sh...  31.4 us
    unnamed x3, local copies, waits for them, and re-layouts  4.86 us
    reduce_sum x1, other arithmetic, tap_rows(): jnp.sum(jnp.where(here[None, None, :, None], taps, 0.0), axis=2)  0.95 us

profile of v1, /device:TPU:11, one launch (start us, length us, event | category | flops | bytes accessed | tf_op | source)
XLA Modules:
  0.0 39.9 jit_solution(6982257560955341383)
XLA Ops:
  1.3 0.7 %bitcast_and_fusion.2 = (pred[2]{0:T(512)(128)(4,1)S(1)}, pred[2]{0:T(512)(128)(4,1)S(1)}, pred[2]{0:T(512)(128)(4,1)S(1)}, pred[2]{0:T(512)(128)(4,1)S(1)}) fusion(s32[]{:T(128)} %bitcast.20, s32[1,2]{1,0:T(1,128)} %param.11), kind=kLoop, calls=%fused_computation.11 | loop fusion | flops 20 | bytes 20 | tf_op jit(solution)/shard_map/and | solution.py:22
  1.9 0.9 %fusion = (f32[9,3,64]{2,1,0:T(4,128)S(1)}, f32[9,3,64]{2,1,0:T(4,128)S(1)}, f32[9,3,64]{2,1,0:T(4,128)S(1)}, f32[9,3,64]{2,1,0:T(4,128)S(1)}) fusion(pred[2]{0:T(512)(128)(4,1)S(1)} %get-tuple-element.16, bf16[1,9,3,2,64]{4,3,2,1,0:T(2,128)(2,1)} %param.9, pred[2]{0:T(512)(128)(4,1)S(1)} %get-tuple-element.14, pred[2]{0:T(512)(128)(4,1)S(1)} %get-tuple-element.15, ...), kind=kLoop, calls=%fused_computation.5 | loop fusion | flops 24192 | bytes 34568 | tf_op jit(solution)/shard_map/reduce_sum | solution.py:23
  2.9 0.1 pad_maximum_fusion
  3.0 0.6 %pad.4.taps_ref = f32[27,512]{1,0:T(8,128)} pad(f32[27,256]{1,0:T(8,128)S(1)} %reshape.68, f32[]{:T(128)} %constant.2.clone.1), padding=0_0x0_256 | pad | bytes 82948 | tf_op jit(solution)/shard_map/jit(_pad)/pad | solution.py:25
  3.7 31.4 %shard_map.85 = (bf16[256,128]{1,0:T(8,128)(2,1)}, bf16[256,128]{1,0:T(8,128)(2,1)}, f32[576,256]{1,0:T(8,128)}) custom-call(f32[27,512]{1,0:T(8,128)} %pad.4.taps_ref, bf16[256,128]{1,0:T(8,128)(2,1)} %bitcast.24, bf16[256,128]{1,0:T(8,128)(2,1)} %bitcast.25, bf16[9,256,256]{2,1,0:T(8,128)(2,1)} %w_ref.1), custom_call_target="tpu_custom_call" | custom-call | flops 8000000000 | bytes 3000000 | tf_op jit(solution)/shard_map/pallas_call | solution.py:293
  35.1 1.5 %copy.13 = bf16[256,1,128]{2,0,1:T(8,128)(2,1)} copy(bf16[256,1,128]{2,0,1:T(8,128)(2,1)} %bitcast.23) | data formatting | bytes 131072
  36.5 1.5 %copy.14 = bf16[256,1,128]{2,0,1:T(8,128)(2,1)} copy(bf16[256,1,128]{2,0,1:T(8,128)(2,1)} %bitcast.22) | data formatting | bytes 131072
  38.0 1.9 %copy.15 = f32[9,64,256]{2,1,0:T(8,128)} copy(f32[9,64,256]{2,1,0:T(8,128)} %bitcast.21) | data formatting | bytes 1179648
  (1 shorter events, 0.0 us)

commit v2 on v1

v2 whole, which is shorter than its diff:
```python
import functools

import jax
import jax.numpy as jnp
from jax import lax
from jax.experimental import pallas as pl
from jax.experimental.pallas import tpu as pltpu
from jax.sharding import PartitionSpec as P

HALO = 128
MESH = pl.DeviceIdType.MESH
NT = (((1,), (1,)), ((), ()))
TN = (((0,), (0,)), ((), ()))


def finish(*refs):
    count = (len(refs) - 1) // 2
    sems = refs[-1]
    copies = [
        pltpu.make_async_copy(refs[i], refs[count + i], sems.at[i]) for i in range(count)
    ]
    for copy in copies:
        copy.start()
    for copy in copies:
        copy.wait()


def kernel(
    n_lat, n_lon, taps_ref, counts_ref, blocks_ref, f_ref, u_ref, w_ref, out_ref, grad_ref, wg_ref,
    f_all, u_all, u_chunk, band, resp, rg, g_mine, g_got,
    part, part_got, chip, result,
    zf_s, zf_r, zc_s, zc_r, zu_s, zu_r, lf_s, lf_r, g_s, g_r, p_s, p_r, x_s, x_r, q_s, q_r,
):
    kernels, channels, _ = w_ref.shape
    width = f_ref.shape[1]
    chunk = u_chunk.shape[1]
    chips = n_lat // 2
    a = lax.axis_index("lat")
    b = lax.axis_index("lon")
    core = lax.rem(a, 2)
    chip_at = a // 2
    twin = a + 1 - 2 * core
    has_up = a < n_lat - 1
    has_down = a > 0

    def lon_peer(step):
        return {"lat": a, "lon": lax.rem(b + step, n_lon)}

    def lat_peer(at):
        return {"lat": at, "lon": b}

    barrier = pltpu.get_barrier_semaphore()
    for step in range(1, n_lon):
        pl.semaphore_signal(barrier, inc=1, device_id=lon_peer(step), device_id_type=MESH)
    for step in range(1, n_lat):
        pl.semaphore_signal(
            barrier, inc=1, device_id=lat_peer(lax.rem(a + step, n_lat)), device_id_type=MESH
        )
    pl.semaphore_wait(barrier, n_lon + n_lat - 2)

    def remote(src, dst, send, recv, to):
        return pltpu.make_async_remote_copy(
            src_ref=src, dst_ref=dst, send_sem=send, recv_sem=recv, device_id=to,
            device_id_type=MESH,
        )

    def send_f(step):
        slot = n_lon - step
        return remote(f_ref, f_all.at[1, slot], zf_s.at[step], zf_r.at[slot], lon_peer(step))

    def send_chunk(step):
        slot = n_lon - step
        start = pl.multiple_of(lax.rem(b + step, n_lon) * chunk, chunk)
        return remote(
            u_ref.at[pl.ds(start, chunk)], u_chunk.at[slot], zc_s.at[step], zc_r.at[slot],
            lon_peer(step),
        )

    def send_u(step):
        slot = n_lon - step
        return remote(u_ref, u_all.at[slot], zu_s.at[step], zu_r.at[slot], lon_peer(step))

    def lat_f(way, slot):
        to = a + 1 if way == 0 else a - 1
        src = f_ref if slot == 0 else f_all.at[1, slot]
        return remote(
            src, f_all.at[2 * way, slot], lf_s.at[way, slot], lf_r.at[way, slot], lat_peer(to)
        )

    steps = sorted(range(1, n_lon), key=lambda step: min(step, n_lon - step), reverse=True)
    for step in steps:
        send_f(step).start()

    @pl.when(has_up)
    def _():
        lat_f(0, 0).start()

    @pl.when(has_down)
    def _():
        lat_f(1, 0).start()

    for step in steps:
        send_chunk(step).start()
    for step in (1, n_lon - 1):
        send_u(step).start()

    slots, block_width = taps_ref.shape[3:]
    lane = lax.broadcasted_iota(jnp.int32, (slots, 4 * HALO), 1)
    which = lax.broadcasted_iota(jnp.int32, (slots, 4 * HALO), 0)
    first = jnp.zeros((slots, 4 * HALO), jnp.int32)
    for s in range(slots):
        first = jnp.where(which == s, HALO + block_width * blocks_ref[0, s], first)
    used = (which < counts_ref[0]) & (lane >= first) & (lane < first + block_width)
    rest = jnp.zeros((slots, 2 * HALO), jnp.float32)
    for k in range(kernels):
        for r in range(3):
            tile = taps_ref[0, k, r].astype(jnp.float32)
            spread = jnp.concatenate([tile] * (2 * HALO // block_width) + [rest], axis=1)
            row = jnp.sum(jnp.where(used, spread, 0.0), axis=0, keepdims=True)
            turned = pltpu.roll(
                jnp.broadcast_to(row, (width, 4 * HALO)), 0, 1, stride=1, stride_axis=0
            ).astype(jnp.bfloat16)
            for d in range(3):
                band[k * width : (k + 1) * width, (3 * d + r) * width : (3 * d + r + 1) * width] = (
                    turned[:, d * width : (d + 1) * width]
                )

    f_all[1, 0] = f_ref[...]

    @pl.when(jnp.logical_not(has_down))
    def _():
        f_all[0] = jnp.zeros(f_all.shape[1:], f_all.dtype)

    @pl.when(jnp.logical_not(has_up))
    def _():
        f_all[2] = jnp.zeros(f_all.shape[1:], f_all.dtype)

    for step in steps[::-1]:
        slot = n_lon - step
        send_f(step).wait_recv()

        @pl.when(has_up)
        def _():
            lat_f(0, slot).start()

        @pl.when(has_down)
        def _():
            lat_f(1, slot).start()

    def wait_lat(slot):
        @pl.when(has_down)
        def _():
            lat_f(0, slot).wait_recv()

        @pl.when(has_up)
        def _():
            lat_f(1, slot).wait_recv()

    group = 3 if kernels % 3 == 0 else 1
    groups = kernels // group

    def convolve(slot):
        window = jnp.concatenate(
            [f_all[r, lax.rem(slot + n_lon - 1 + d, n_lon)] for d in range(3) for r in range(3)],
            axis=1,
        )
        for k0 in range(0, kernels, group):
            got = lax.dot_general(
                window, band[k0 * width : (k0 + group) * width, :], NT,
                preferred_element_type=jnp.float32,
            ).astype(jnp.bfloat16)
            for k in range(group):
                resp[k0 + k, slot] = got[:, k * width : (k + 1) * width]

    for slot in (0, 1, n_lon - 1):
        wait_lat(slot)
    convolve(0)
    for slot in range(2, n_lon - 1):
        wait_lat(slot)
    pl.loop(1, n_lon)(convolve)

    u_chunk[0] = u_ref[pl.ds(pl.multiple_of(b * chunk, chunk), chunk), :]
    for step in range(1, n_lon):
        send_chunk(step).wait_recv()
    u_line = jnp.concatenate([u_chunk[slot] for slot in range(n_lon)], axis=1)

    def send_p(g):
        return remote(
            part.at[1 - core, g], part_got.at[g], p_s.at[g], p_r.at[g], lat_peer(twin)
        )

    for g in range(groups):
        for k in range(group):
            line = jnp.concatenate(
                [resp[g * group + k, slot] for slot in range(n_lon)], axis=1
            )
            piece = lax.dot_general(u_line, line, NT, preferred_element_type=jnp.float32)
            for half in range(2):
                part[half, g, k * chunk : (k + 1) * chunk, :] = piece[
                    :, half * channels // 2 : (half + 1) * channels // 2
                ]
        send_p(g).start()

    def send_x(g, step):
        to = lax.rem(a + 2 * step, n_lat)
        return remote(
            chip.at[chip_at, g], chip.at[chip_at, g], x_s.at[g, step],
            x_r.at[g, chips - step], lat_peer(to),
        )

    def got_x(g, step):
        at = lax.rem(chip_at + chips - step, chips)
        return remote(
            chip.at[at, g], chip.at[at, g], x_s.at[g, step], x_r.at[g, chips - step],
            lat_peer(twin),
        )

    for g in range(groups):
        send_p(g).wait_recv()
        chip[chip_at, g] = (part[core, g] + part_got[g]).astype(chip.dtype)
        for step in range(1, chips):
            send_x(g, step).start()

    u_all[0] = u_ref[...]
    for step in (1, n_lon - 1):
        send_u(step).wait_recv()
    u_wide = jnp.concatenate([u_all[n_lon - 1], u_all[0], u_all[1]], axis=1)
    for k in range(kernels):
        mixed = lax.dot_general(
            w_ref[k], u_wide, TN, preferred_element_type=jnp.float32
        ).astype(jnp.bfloat16)
        for j in range(3):
            rg[j, :, k * width : (k + 1) * width] = mixed[:, j * width : (j + 1) * width]
    terms = jnp.zeros((channels, 3 * width), jnp.float32)
    for j in range(3):
        terms = terms + jnp.dot(
            rg[j], band[:, (2 - j) * 3 * width : (3 - j) * 3 * width],
            preferred_element_type=jnp.float32,
        )
    for r in range(3):
        g_mine[r] = terms[:, r * width : (r + 1) * width]

    def send_g(way):
        to = a + 1 if way == 0 else a - 1
        return remote(g_mine.at[2 - 2 * way], g_got.at[way], g_s.at[way], g_r.at[way], lat_peer(to))

    @pl.when(has_up)
    def _():
        send_g(0).start()

    @pl.when(has_down)
    def _():
        send_g(1).start()

    mixed = jnp.zeros((channels, width), jnp.float32)
    for k in range(kernels):
        mixed = mixed + jnp.dot(w_ref[k], resp[k, 0], preferred_element_type=jnp.float32)
    out_ref[...] = mixed.astype(out_ref.dtype)

    def send_q(g):
        return remote(result.at[core, g], result.at[core, g], q_s.at[g], q_r.at[g], lat_peer(twin))

    def got_q(g):
        return remote(
            result.at[1 - core, g], result.at[1 - core, g], q_s.at[g], q_r.at[g], lat_peer(twin)
        )

    for g in range(groups):
        for step in range(1, chips):
            got_x(g, step).wait_recv()
        total = chip[0, g].astype(jnp.float32)
        for at in range(1, chips):
            total = total + chip[at, g].astype(jnp.float32)
        result[core, g] = total
        send_q(g).start()

    @pl.when(has_down)
    def _():
        send_g(0).wait_recv()

    @pl.when(has_up)
    def _():
        send_g(1).wait_recv()

    below = jnp.where(has_down, g_got[0], 0.0)
    above = jnp.where(has_up, g_got[1], 0.0)
    grad_ref[...] = (g_mine[1] + below + above).astype(grad_ref.dtype)

    for g in range(groups):
        got_q(g).wait_recv()
        rows = slice(g * group * chunk, (g + 1) * group * chunk)
        wg_ref[rows, : channels // 2] = result[0, g]
        wg_ref[rows, channels // 2 :] = result[1, g]

    for step in range(1, n_lon):
        send_f(step).wait_send()
        send_chunk(step).wait_send()
    for step in (1, n_lon - 1):
        send_u(step).wait_send()
    for slot in range(n_lon):
        @pl.when(has_up)
        def _():
            lat_f(0, slot).wait_send()

        @pl.when(has_down)
        def _():
            lat_f(1, slot).wait_send()

    @pl.when(has_up)
    def _():
        send_g(0).wait_send()

    @pl.when(has_down)
    def _():
        send_g(1).wait_send()

    for g in range(groups):
        send_p(g).wait_send()
        for step in range(1, chips):
            send_x(g, step).wait_send()
        send_q(g).wait_send()


def body(fields, upstream, weights, filter_taps, cycle_counts, cycle_blocks):
    channels, _, width = fields.shape
    kernels = weights.shape[0]
    n_lat, n_lon = lax.axis_size("lat"), lax.axis_size("lon")
    chunk = channels // n_lon
    groups = kernels // 3 if kernels % 3 == 0 else kernels
    rows, half = kernels // groups * chunk, channels // 2
    bf16, f32 = jnp.bfloat16, jnp.float32
    dma = pltpu.SemaphoreType.DMA
    vmem = pl.BlockSpec(memory_space=pltpu.VMEM)
    smem = pl.BlockSpec(memory_space=pltpu.SMEM)
    anywhere = pl.BlockSpec(memory_space=pl.ANY)
    results = pl.pallas_call(
        functools.partial(kernel, n_lat, n_lon),
        out_shape=(
            jax.ShapeDtypeStruct((channels, width), bf16),
            jax.ShapeDtypeStruct((channels, width), bf16),
            jax.ShapeDtypeStruct((kernels * chunk, channels), f32),
        ),
        in_specs=[vmem, smem, smem, vmem, vmem, vmem],
        out_specs=[vmem] * 3,
        scratch_shapes=[
            pltpu.VMEM((3, n_lon, channels, width), bf16),
            pltpu.VMEM((n_lon, channels, width), bf16),
            pltpu.VMEM((n_lon, chunk, width), bf16),
            pltpu.VMEM((kernels * width, 9 * width), bf16),
            pltpu.VMEM((kernels, n_lon, channels, width), bf16),
            pltpu.VMEM((3, channels, kernels * width), bf16),
            pltpu.VMEM((3, channels, width), f32),
            pltpu.VMEM((2, channels, width), f32),
            pltpu.VMEM((2, groups, rows, half), f32),
            pltpu.VMEM((groups, rows, half), f32),
            pltpu.VMEM((n_lat // 2, groups, rows, half), bf16),
            pltpu.VMEM((2, groups, rows, half), f32),
            dma((n_lon,)), dma((n_lon,)), dma((n_lon,)), dma((n_lon,)), dma((n_lon,)), dma((n_lon,)),
            dma((2, n_lon)), dma((2, n_lon)), dma((2,)), dma((2,)),
            dma((groups,)), dma((groups,)), dma((groups, n_lat // 2)), dma((groups, n_lat // 2 + 1)),
            dma((groups,)), dma((groups,)),
        ],
        compiler_params=pltpu.CompilerParams(
            collective_id=0, has_side_effects=True, vmem_limit_bytes=56 * 1024 * 1024
        ),
        cost_estimate=pl.CostEstimate(
            flops=8_000_000_000, bytes_accessed=3_000_000, transcendentals=0
        ),
    )(
        filter_taps, cycle_counts, cycle_blocks,
        fields.reshape(channels, width), upstream.reshape(channels, width), weights,
    )
    outputs, grad, weight_grad = pl.pallas_call(
        finish,
        out_shape=tuple(jax.ShapeDtypeStruct(held.shape, held.dtype) for held in results),
        in_specs=[anywhere] * 3,
        out_specs=[anywhere] * 3,
        scratch_shapes=[dma((3,))],
        compiler_params=pltpu.CompilerParams(vmem_limit_bytes=56 * 1024 * 1024),
    )(*results)
    return (
        outputs.reshape(fields.shape),
        grad.reshape(fields.shape),
        weight_grad.reshape(kernels, chunk, channels),
    )


def solution(mesh):
    return jax.shard_map(
        body,
        mesh=mesh,
        in_specs=(
            P("groups", "lat", "lon"),
            P("groups", "lat", "lon"),
            P(),
            P("lat", None, None, None, None),
            P("lat"),
            P("lat", None),
        ),
        out_specs=(P("groups", "lat", "lon"), P("groups", "lat", "lon"), P("groups", "lon", None)),
        check_vma=False,
    )
```

time: 40.3 us -> 56.2 us (1.39)
  Pallas kernels: 31.4 us -> 54.8 us
  local copies, waits for them, and re-layouts: 5.51 us -> 0 us
  other arithmetic: 1.71 us -> 0 us
    pallas_call x0 -> x1, Pallas kernels: none -> 23 us  [body(): pl.pallas_call(finish, out_shape=tuple((jax.ShapeDtypeStruct(held.shape,...]
    unnamed x3 -> x0, local copies, waits for them, and re-layouts: 4.86 us -> none
    reduce_sum x1 -> x0, other arithmetic: 0.95 us -> none  [tap_rows(): jnp.sum(jnp.where(here[None, None, :, None], taps, 0.0), axis=2)]
    and x1 -> x0, other arithmetic: 0.66 us -> none  [tap_rows(): here = live & (cycle_blocks[0] + HALO // width == block)]
    pad x1 -> x0, local copies, waits for them, and re-layouts: 0.64 us -> none  [tap_rows(): return jnp.pad(table, ((0, 0), (0, 2 * HALO)))]
where the time goes in v2:
time: 56.2 us; the launch traced here: 56 us
  Pallas kernels  54.8 us (98%)
  between operations  1.29 us (2%)
    pallas_call x1, Pallas kernels, body(): pl.pallas_call(functools.partial(kernel, n_lat, n_lon), out_shape=(jax.Sh...  31.8 us
    pallas_call x1, Pallas kernels, body(): pl.pallas_call(finish, out_shape=tuple((jax.ShapeDtypeStruct(held.shape,...  23 us

profile of v2, /device:TPU:11, one launch (start us, length us, event | category | flops | bytes accessed | tf_op | source)
XLA Modules:
  0.0 56.0 jit_solution(12373435178586877105)
XLA Ops:
  1.3 31.8 %shard_map.85 = (bf16[256,128]{1,0:T(8,128)(2,1)}, bf16[256,128]{1,0:T(8,128)(2,1)}, f32[576,256]{1,0:T(8,128)}) custom-call(bf16[1,9,3,2,64]{4,3,2,1,0:T(2,128)(2,1)} %taps_ref.1, s32[1]{0:T(128)S(6)} %copy.9.counts_ref, s32[1,2]{1,0:T(1,128)} %blocks_ref.1, bf16[256,128]{1,0:T(8,128)(2,1)} %bitcast.6, bf16[256,128]{1,0:T(8,128)(2,1)} %bitcast.7, ...), custom_call_target="tpu_custom_call" | custom-call | flops 8000000000 | bytes 3000000 | tf_op jit(solution)/shard_map/pallas_call | solution.py:336
  33.1 23.0 %shard_map.86 = (bf16[256,128]{1,0:T(8,128)(2,1)}, bf16[256,128]{1,0:T(8,128)(2,1)}, f32[576,256]{1,0:T(8,128)}) custom-call(bf16[256,128]{1,0:T(8,128)(2,1)} %get-tuple-element.9.refs_0_, bf16[256,128]{1,0:T(8,128)(2,1)} %get-tuple-element.10.refs_1_, f32[576,256]{1,0:T(8,128)} %get-tuple-element.11.refs_2_), custom_call_target="tpu_custom_call" | custom-call | tf_op jit(solution)/shard_map/pallas_call | solution.py:373

commit v3 on v2

--- a/solution.py
+++ b/solution.py
@@ -9,27 +9,19 @@
 
 HALO = 128
 MESH = pl.DeviceIdType.MESH
-NT = (((1,), (1,)), ((), ()))
-TN = (((0,), (0,)), ((), ()))
 
 
 def finish(*refs):
-    count = (len(refs) - 1) // 2
-    sems = refs[-1]
-    copies = [
-        pltpu.make_async_copy(refs[i], refs[count + i], sems.at[i]) for i in range(count)
-    ]
-    for copy in copies:
-        copy.start()
-    for copy in copies:
-        copy.wait()
+    count = len(refs) // 2
+    for i in range(count):
+        refs[count + i][...] = refs[i][...]
 
 
 def kernel(
-    n_lat, n_lon, taps_ref, counts_ref, blocks_ref, f_ref, u_ref, w_ref, out_ref, grad_ref, wg_ref,
-    f_all, u_all, u_chunk, band, resp, rg, g_mine, g_got,
+    n_lat, n_lon, taps_ref, counts_ref, blocks_ref, f_ref, u_ref, w_hbm, out_ref, grad_ref, wg_ref,
+    w_ref, w_turned, f_mine, f_all, u_all, u_chunk, band, resp, rg, g_mine, g_got,
     part, part_got, chip, result,
-    zf_s, zf_r, zc_s, zc_r, zu_s, zu_r, lf_s, lf_r, g_s, g_r, p_s, p_r, x_s, x_r, q_s, q_r,
+    zf_s, zf_r, zc_s, zc_r, zu_s, zu_r, lf_s, lf_r, g_s, g_r, p_s, p_r, x_s, x_r, q_s, q_r, w_s,
 ):
     kernels, channels, _ = w_ref.shape
     width = f_ref.shape[1]
@@ -49,6 +41,8 @@
     def lat_peer(at):
         return {"lat": at, "lon": b}
 
+    load_w = pltpu.make_async_copy(w_hbm, w_ref, w_s)
+    load_w.start()
     barrier = pltpu.get_barrier_semaphore()
     for step in range(1, n_lon):
         pl.semaphore_signal(barrier, inc=1, device_id=lon_peer(step), device_id_type=MESH)
@@ -56,6 +50,7 @@
         pl.semaphore_signal(
             barrier, inc=1, device_id=lat_peer(lax.rem(a + step, n_lat)), device_id_type=MESH
         )
+    f_mine[...] = f_ref[...].T
     pl.semaphore_wait(barrier, n_lon + n_lat - 2)
 
     def remote(src, dst, send, recv, to):
@@ -66,7 +61,7 @@
 
     def send_f(step):
         slot = n_lon - step
-        return remote(f_ref, f_all.at[1, slot], zf_s.at[step], zf_r.at[slot], lon_peer(step))
+        return remote(f_mine, f_all.at[slot, 1], zf_s.at[step], zf_r.at[slot], lon_peer(step))
 
     def send_chunk(step):
         slot = n_lon - step
@@ -82,9 +77,9 @@
 
     def lat_f(way, slot):
         to = a + 1 if way == 0 else a - 1
-        src = f_ref if slot == 0 else f_all.at[1, slot]
-        return remote(
-            src, f_all.at[2 * way, slot], lf_s.at[way, slot], lf_r.at[way, slot], lat_peer(to)
+        src = f_mine if slot == 0 else f_all.at[slot, 1]
+        return remote(
+            src, f_all.at[slot, 2 * way], lf_s.at[way, slot], lf_r.at[way, slot], lat_peer(to)
         )
 
     steps = sorted(range(1, n_lon), key=lambda step: min(step, n_lon - step), reverse=True)
@@ -101,8 +96,6 @@
 
     for step in steps:
         send_chunk(step).start()
-    for step in (1, n_lon - 1):
-        send_u(step).start()
 
     slots, block_width = taps_ref.shape[3:]
     lane = lax.broadcasted_iota(jnp.int32, (slots, 4 * HALO), 1)
@@ -125,15 +118,19 @@
                     turned[:, d * width : (d + 1) * width]
                 )
 
-    f_all[1, 0] = f_ref[...]
+    load_w.wait()
+    for k in range(kernels):
+        w_turned[k * channels : (k + 1) * channels, :] = w_ref[k].T
+
+    f_all[0, 1] = f_mine[...]
 
     @pl.when(jnp.logical_not(has_down))
     def _():
-        f_all[0] = jnp.zeros(f_all.shape[1:], f_all.dtype)
+        f_all[:, 0] = jnp.zeros((n_lon, width, channels), f_all.dtype)
 
     @pl.when(jnp.logical_not(has_up))
     def _():
-        f_all[2] = jnp.zeros(f_all.shape[1:], f_all.dtype)
+        f_all[:, 2] = jnp.zeros((n_lon, width, channels), f_all.dtype)
 
     for step in steps[::-1]:
         slot = n_lon - step
@@ -147,6 +144,9 @@
         def _():
             lat_f(1, slot).start()
 
+    for step in (1, n_lon - 1):
+        send_u(step).start()
+
     def wait_lat(slot):
         @pl.when(has_down)
         def _():
@@ -161,16 +161,16 @@
 
     def convolve(slot):
         window = jnp.concatenate(
-            [f_all[r, lax.rem(slot + n_lon - 1 + d, n_lon)] for d in range(3) for r in range(3)],
-            axis=1,
+            [f_all[lax.rem(slot + n_lon - 1 + d, n_lon), r] for d in range(3) for r in range(3)],
+            axis=0,
         )
         for k0 in range(0, kernels, group):
-            got = lax.dot_general(
-                window, band[k0 * width : (k0 + group) * width, :], NT,
+            got = jnp.dot(
+                band[k0 * width : (k0 + group) * width, :], window,
                 preferred_element_type=jnp.float32,
             ).astype(jnp.bfloat16)
             for k in range(group):
-                resp[k0 + k, slot] = got[:, k * width : (k + 1) * width]
+                resp[k0 + k, slot] = got[k * width : (k + 1) * width]
 
     for slot in (0, 1, n_lon - 1):
         wait_lat(slot)
@@ -191,10 +191,8 @@
 
     for g in range(groups):
         for k in range(group):
-            line = jnp.concatenate(
-                [resp[g * group + k, slot] for slot in range(n_lon)], axis=1
-            )
-            piece = lax.dot_general(u_line, line, NT, preferred_element_type=jnp.float32)
+            line = resp[g * group + k].reshape(n_lon * width, channels)
+            piece = jnp.dot(u_line, line, preferred_element_type=jnp.float32)
             for half in range(2):
                 part[half, g, k * chunk : (k + 1) * chunk, :] = piece[
                     :, half * channels // 2 : (half + 1) * channels // 2
@@ -226,8 +224,9 @@
         send_u(step).wait_recv()
     u_wide = jnp.concatenate([u_all[n_lon - 1], u_all[0], u_all[1]], axis=1)
     for k in range(kernels):
-        mixed = lax.dot_general(
-            w_ref[k], u_wide, TN, preferred_element_type=jnp.float32
+        mixed = jnp.dot(
+            w_turned[k * channels : (k + 1) * channels, :], u_wide,
+            preferred_element_type=jnp.float32,
         ).astype(jnp.bfloat16)
         for j in range(3):
             rg[j, :, k * width : (k + 1) * width] = mixed[:, j * width : (j + 1) * width]
@@ -252,10 +251,9 @@
     def _():
         send_g(1).start()
 
-    mixed = jnp.zeros((channels, width), jnp.float32)
-    for k in range(kernels):
-        mixed = mixed + jnp.dot(w_ref[k], resp[k, 0], preferred_element_type=jnp.float32)
-    out_ref[...] = mixed.astype(out_ref.dtype)
+    here = jnp.concatenate([resp[k, 0] for k in range(kernels)], axis=1)
+    mixed = jnp.dot(here, w_turned[...], preferred_element_type=jnp.float32)
+    out_ref[...] = mixed.astype(out_ref.dtype).T
 
     def send_q(g):
         return remote(result.at[core, g], result.at[core, g], q_s.at[g], q_r.at[g], lat_peer(twin))
@@ -340,14 +338,17 @@
             jax.ShapeDtypeStruct((channels, width), bf16),
             jax.ShapeDtypeStruct((kernels * chunk, channels), f32),
         ),
-        in_specs=[vmem, smem, smem, vmem, vmem, vmem],
+        in_specs=[vmem, smem, smem, vmem, vmem, anywhere],
         out_specs=[vmem] * 3,
         scratch_shapes=[
-            pltpu.VMEM((3, n_lon, channels, width), bf16),
+            pltpu.VMEM(weights.shape, bf16),
+            pltpu.VMEM((kernels * channels, channels), bf16),
+            pltpu.VMEM((width, channels), bf16),
+            pltpu.VMEM((n_lon, 3, width, channels), bf16),
             pltpu.VMEM((n_lon, channels, width), bf16),
             pltpu.VMEM((n_lon, chunk, width), bf16),
             pltpu.VMEM((kernels * width, 9 * width), bf16),
-            pltpu.VMEM((kernels, n_lon, channels, width), bf16),
+            pltpu.VMEM((kernels, n_lon, width, channels), bf16),
             pltpu.VMEM((3, channels, kernels * width), bf16),
             pltpu.VMEM((3, channels, width), f32),
             pltpu.VMEM((2, channels, width), f32),
@@ -358,7 +359,7 @@
             dma((n_lon,)), dma((n_lon,)), dma((n_lon,)), dma((n_lon,)), dma((n_lon,)), dma((n_lon,)),
             dma((2, n_lon)), dma((2, n_lon)), dma((2,)), dma((2,)),
             dma((groups,)), dma((groups,)), dma((groups, n_lat // 2)), dma((groups, n_lat // 2 + 1)),
-            dma((groups,)), dma((groups,)),
+            dma((groups,)), dma((groups,)), dma,
         ],
         compiler_params=pltpu.CompilerParams(
             collective_id=0, has_side_effects=True, vmem_limit_bytes=56 * 1024 * 1024
@@ -373,10 +374,8 @@
     outputs, grad, weight_grad = pl.pallas_call(
         finish,
         out_shape=tuple(jax.ShapeDtypeStruct(held.shape, held.dtype) for held in results),
-        in_specs=[anywhere] * 3,
-        out_specs=[anywhere] * 3,
-        scratch_shapes=[dma((3,))],
-        compiler_params=pltpu.CompilerParams(vmem_limit_bytes=56 * 1024 * 1024),
+        in_specs=[vmem] * 3,
+        out_specs=[vmem] * 3,
     )(*results)
     return (
         outputs.reshape(fields.shape),

time: 56.2 us -> 32.4 us (0.58)
  the two profiles are of different devices: /device:TPU:11 before, /device:TPU:15 now
where the time goes in v3:
time: 32.4 us; the launch traced here: 32.2 us
  Pallas kernels  30.9 us (95%)
  between operations  1.29 us (4%)
    pallas_call x1, Pallas kernels, body(): pl.pallas_call(functools.partial(kernel, n_lat, n_lon), out_shape=(jax.Sh...  28.9 us
    pallas_call x1, Pallas kernels, body(): pl.pallas_call(finish, out_shape=tuple((jax.ShapeDtypeStruct(held.shape,...  2.01 us

profile of v3, /device:TPU:15, one launch (start us, length us, event | category | flops | bytes accessed | tf_op | source)
XLA Modules:
  0.0 32.2 jit_solution(13418756238258126677)
XLA Ops:
  1.3 28.9 %shard_map.85 = (bf16[256,128]{1,0:T(8,128)(2,1)}, bf16[256,128]{1,0:T(8,128)(2,1)}, f32[576,256]{1,0:T(8,128)}) custom-call(bf16[1,9,3,2,64]{4,3,2,1,0:T(2,128)(2,1)} %taps_ref.1, s32[1]{0:T(128)S(6)} %copy.9.counts_ref, s32[1,2]{1,0:T(1,128)} %blocks_ref.1, bf16[256,128]{1,0:T(8,128)(2,1)} %bitcast.6, bf16[256,128]{1,0:T(8,128)(2,1)} %bitcast.7, ...), custom_call_target="tpu_custom_call" | custom-call | flops 8000000000 | bytes 3000000 | tf_op jit(solution)/shard_map/pallas_call | solution.py:334
  30.2 2.0 %shard_map.86 = (bf16[256,128]{1,0:T(8,128)(2,1)}, bf16[256,128]{1,0:T(8,128)(2,1)}, f32[576,256]{1,0:T(8,128)}) custom-call(bf16[256,128]{1,0:T(8,128)(2,1)} %get-tuple-element.9.refs_0_, bf16[256,128]{1,0:T(8,128)(2,1)} %get-tuple-element.10.refs_1_, f32[576,256]{1,0:T(8,128)} %get-tuple-element.11.refs_2_), custom_call_target="tpu_custom_call" | custom-call | tf_op jit(solution)/shard_map/pallas_call | solution.py:374

commit v4 on v3

--- a/solution.py
+++ b/solution.py
@@ -19,7 +19,7 @@
 
 def kernel(
     n_lat, n_lon, taps_ref, counts_ref, blocks_ref, f_ref, u_ref, w_hbm, out_ref, grad_ref, wg_ref,
-    w_ref, w_turned, f_mine, f_all, u_all, u_chunk, band, resp, rg, g_mine, g_got,
+    w_ref, w_turned, f_mine, f_all, u_all, u_chunk, band, resp, met, rg, g_mine, g_got,
     part, part_got, chip, result,
     zf_s, zf_r, zc_s, zc_r, zu_s, zu_r, lf_s, lf_r, g_s, g_r, p_s, p_r, x_s, x_r, q_s, q_r, w_s,
 ):
@@ -82,7 +82,9 @@
             src, f_all.at[slot, 2 * way], lf_s.at[way, slot], lf_r.at[way, slot], lat_peer(to)
         )
 
-    steps = sorted(range(1, n_lon), key=lambda step: min(step, n_lon - step), reverse=True)
+    steps = sorted(range(1, n_lon), key=lambda step: min(step, n_lon - step))
+    for step in steps:
+        send_chunk(step).start()
     for step in steps:
         send_f(step).start()
 
@@ -93,9 +95,6 @@
     @pl.when(has_down)
     def _():
         lat_f(1, 0).start()
-
-    for step in steps:
-        send_chunk(step).start()
 
     slots, block_width = taps_ref.shape[3:]
     lane = lax.broadcasted_iota(jnp.int32, (slots, 4 * HALO), 1)
@@ -118,35 +117,54 @@
                     turned[:, d * width : (d + 1) * width]
                 )
 
+    f_all[0, 1] = f_mine[...]
+
+    @pl.when(jnp.logical_not(has_down))
+    def _():
+        f_all[:, 0] = jnp.zeros((n_lon, width, channels), f_all.dtype)
+
+    @pl.when(jnp.logical_not(has_up))
+    def _():
+        f_all[:, 2] = jnp.zeros((n_lon, width, channels), f_all.dtype)
+
+    u_chunk[0] = u_ref[pl.ds(pl.multiple_of(b * chunk, chunk), chunk), :]
+    for step in steps:
+        send_chunk(step).wait_recv()
+    lines = jnp.concatenate(
+        [
+            jnp.concatenate([u_chunk[(slot + 1 - d) % n_lon] for d in range(3)], axis=1)
+            for slot in range(n_lon)
+        ],
+        axis=0,
+    )
+    for k in range(kernels):
+        rows = slice(k * width, (k + 1) * width)
+        taps_k = jnp.concatenate(
+            [band[rows, 3 * d * width : 3 * (d + 1) * width] for d in range(3)], axis=0
+        )
+        spread = jnp.dot(lines, taps_k, preferred_element_type=jnp.float32).astype(jnp.bfloat16)
+        for slot in range(n_lon):
+            met[slot, k * chunk : (k + 1) * chunk, :] = spread[slot * chunk : (slot + 1) * chunk]
+
+    for step in steps:
+        slot = n_lon - step
+        send_f(step).wait_recv()
+
+        @pl.when(has_up)
+        def _():
+            lat_f(0, slot).start()
+
+        @pl.when(has_down)
+        def _():
+            lat_f(1, slot).start()
+
+    for step in (1, n_lon - 1):
+        send_u(step).start()
+
     load_w.wait()
     for k in range(kernels):
         w_turned[k * channels : (k + 1) * channels, :] = w_ref[k].T
 
-    f_all[0, 1] = f_mine[...]
-
-    @pl.when(jnp.logical_not(has_down))
-    def _():
-        f_all[:, 0] = jnp.zeros((n_lon, width, channels), f_all.dtype)
-
-    @pl.when(jnp.logical_not(has_up))
-    def _():
-        f_all[:, 2] = jnp.zeros((n_lon, width, channels), f_all.dtype)
-
-    for step in steps[::-1]:
-        slot = n_lon - step
-        send_f(step).wait_recv()
-
-        @pl.when(has_up)
-        def _():
-            lat_f(0, slot).start()
-
-        @pl.when(has_down)
-        def _():
-            lat_f(1, slot).start()
-
-    for step in (1, n_lon - 1):
-        send_u(step).start()
-
     def wait_lat(slot):
         @pl.when(has_down)
         def _():
@@ -159,30 +177,21 @@
     group = 3 if kernels % 3 == 0 else 1
     groups = kernels // group
 
-    def convolve(slot):
-        window = jnp.concatenate(
-            [f_all[lax.rem(slot + n_lon - 1 + d, n_lon), r] for d in range(3) for r in range(3)],
-            axis=0,
-        )
-        for k0 in range(0, kernels, group):
-            got = jnp.dot(
-                band[k0 * width : (k0 + group) * width, :], window,
-                preferred_element_type=jnp.float32,
-            ).astype(jnp.bfloat16)
-            for k in range(group):
-                resp[k0 + k, slot] = got[k * width : (k + 1) * width]
-
-    for slot in (0, 1, n_lon - 1):
+    order = [0] + [n_lon - step for step in steps]
+    total = jnp.zeros((kernels * chunk, channels), jnp.float32)
+    for slot in order[:-1]:
         wait_lat(slot)
-    convolve(0)
-    for slot in range(2, n_lon - 1):
-        wait_lat(slot)
-    pl.loop(1, n_lon)(convolve)
-
-    u_chunk[0] = u_ref[pl.ds(pl.multiple_of(b * chunk, chunk), chunk), :]
-    for step in range(1, n_lon):
-        send_chunk(step).wait_recv()
-    u_line = jnp.concatenate([u_chunk[slot] for slot in range(n_lon)], axis=1)
+        total = total + jnp.dot(
+            met[slot], f_all[slot].reshape(3 * width, channels),
+            preferred_element_type=jnp.float32,
+        )
+    for g in range(groups):
+        for half in range(2):
+            part[half, g] = total[
+                g * group * chunk : (g + 1) * group * chunk,
+                half * channels // 2 : (half + 1) * channels // 2,
+            ]
+    wait_lat(order[-1])
 
     def send_p(g):
         return remote(
@@ -190,14 +199,28 @@
         )
 
     for g in range(groups):
+        piece = jnp.dot(
+            met[order[-1], g * group * chunk : (g + 1) * group * chunk, :],
+            f_all[order[-1]].reshape(3 * width, channels),
+            preferred_element_type=jnp.float32,
+        )
+        for half in range(2):
+            part[half, g] += piece[:, half * channels // 2 : (half + 1) * channels // 2]
+        send_p(g).start()
+
+    window = jnp.concatenate(
+        [f_all[slot].reshape(3 * width, channels) for slot in (n_lon - 1, 0, 1)], axis=0
+    )
+
+    def convolve(g):
+        got = jnp.dot(
+            band[g * group * width : (g + 1) * group * width, :], window,
+            preferred_element_type=jnp.float32,
+        ).astype(jnp.bfloat16)
         for k in range(group):
-            line = resp[g * group + k].reshape(n_lon * width, channels)
-            piece = jnp.dot(u_line, line, preferred_element_type=jnp.float32)
-            for half in range(2):
-                part[half, g, k * chunk : (k + 1) * chunk, :] = piece[
-                    :, half * channels // 2 : (half + 1) * channels // 2
-                ]
-        send_p(g).start()
+            resp[:, (g * group + k) * channels : (g * group + k + 1) * channels] = got[
+                k * width : (k + 1) * width
+            ]
 
     def send_x(g, step):
         to = lax.rem(a + 2 * step, n_lat)
@@ -214,6 +237,7 @@
         )
 
     for g in range(groups):
+        convolve(g)
         send_p(g).wait_recv()
         chip[chip_at, g] = (part[core, g] + part_got[g]).astype(chip.dtype)
         for step in range(1, chips):
@@ -251,8 +275,7 @@
     def _():
         send_g(1).start()
 
-    here = jnp.concatenate([resp[k, 0] for k in range(kernels)], axis=1)
-    mixed = jnp.dot(here, w_turned[...], preferred_element_type=jnp.float32)
+    mixed = jnp.dot(resp[...], w_turned[...], preferred_element_type=jnp.float32)
     out_ref[...] = mixed.astype(out_ref.dtype).T
 
     def send_q(g):
@@ -348,7 +371,8 @@
             pltpu.VMEM((n_lon, channels, width), bf16),
             pltpu.VMEM((n_lon, chunk, width), bf16),
             pltpu.VMEM((kernels * width, 9 * width), bf16),
-            pltpu.VMEM((kernels, n_lon, width, channels), bf16),
+            pltpu.VMEM((width, kernels * channels), bf16),
+            pltpu.VMEM((n_lon, kernels * chunk, 3 * width), bf16),
             pltpu.VMEM((3, channels, kernels * width), bf16),
             pltpu.VMEM((3, channels, width), f32),
             pltpu.VMEM((2, channels, width), f32),

time: 32.4 us -> 30.5 us (0.941)
  the two profiles are of different devices: /device:TPU:15 before, /device:TPU:1 now
where the time goes in v4:
time: 30.5 us; the launch traced here: 30.3 us
  Pallas kernels  29 us (95%)
  between operations  1.29 us (4%)
    pallas_call x1, Pallas kernels, body(): pl.pallas_call(functools.partial(kernel, n_lat, n_lon), out_shape=(jax.Sh...  27 us
    pallas_call x1, Pallas kernels, body(): pl.pallas_call(finish, out_shape=tuple((jax.ShapeDtypeStruct(held.shape,...  2.01 us

profile of v4, /device:TPU:1, one launch (start us, length us, event | category | flops | bytes accessed | tf_op | source)
XLA Modules:
  0.0 30.3 jit_solution(16385183467043095554)
XLA Ops:
  1.3 27.0 %shard_map.85 = (bf16[256,128]{1,0:T(8,128)(2,1)}, bf16[256,128]{1,0:T(8,128)(2,1)}, f32[576,256]{1,0:T(8,128)}) custom-call(bf16[1,9,3,2,64]{4,3,2,1,0:T(2,128)(2,1)} %taps_ref.1, s32[1]{0:T(128)S(6)} %copy.9.counts_ref, s32[1,2]{1,0:T(1,128)} %blocks_ref.1, bf16[256,128]{1,0:T(8,128)(2,1)} %bitcast.6, bf16[256,128]{1,0:T(8,128)(2,1)} %bitcast.7, ...), custom_call_target="tpu_custom_call" | custom-call | flops 8000000000 | bytes 3000000 | tf_op jit(solution)/shard_map/pallas_call | solution.py:357
  28.3 2.0 %shard_map.86 = (bf16[256,128]{1,0:T(8,128)(2,1)}, bf16[256,128]{1,0:T(8,128)(2,1)}, f32[576,256]{1,0:T(8,128)}) custom-call(bf16[256,128]{1,0:T(8,128)(2,1)} %get-tuple-element.9.refs_0_, bf16[256,128]{1,0:T(8,128)(2,1)} %get-tuple-element.10.refs_1_, f32[576,256]{1,0:T(8,128)} %get-tuple-element.11.refs_2_), custom_call_target="tpu_custom_call" | custom-call | tf_op jit(solution)/shard_map/pallas_call | solution.py:398

commit v5 on v4

--- a/solution.py
+++ b/solution.py
@@ -109,8 +109,11 @@
             tile = taps_ref[0, k, r].astype(jnp.float32)
             spread = jnp.concatenate([tile] * (2 * HALO // block_width) + [rest], axis=1)
             row = jnp.sum(jnp.where(used, spread, 0.0), axis=0, keepdims=True)
-            turned = pltpu.roll(
-                jnp.broadcast_to(row, (width, 4 * HALO)), 0, 1, stride=1, stride_axis=0
+            eight = pltpu.roll(
+                jnp.broadcast_to(row, (8, 4 * HALO)), 0, 1, stride=1, stride_axis=0
+            )
+            turned = jnp.concatenate(
+                [eight if p == 0 else pltpu.roll(eight, p, 1) for p in range(0, width, 8)], axis=0
             ).astype(jnp.bfloat16)
             for d in range(3):
                 band[k * width : (k + 1) * width, (3 * d + r) * width : (3 * d + r + 1) * width] = (
@@ -126,6 +129,21 @@
     @pl.when(jnp.logical_not(has_up))
     def _():
         f_all[:, 2] = jnp.zeros((n_lon, width, channels), f_all.dtype)
+
+    for step in steps:
+        slot = n_lon - step
+        send_f(step).wait_recv()
+
+        @pl.when(has_up)
+        def _():
+            lat_f(0, slot).start()
+
+        @pl.when(has_down)
+        def _():
+            lat_f(1, slot).start()
+
+    for step in (1, n_lon - 1):
+        send_u(step).start()
 
     u_chunk[0] = u_ref[pl.ds(pl.multiple_of(b * chunk, chunk), chunk), :]
     for step in steps:
@@ -145,21 +163,6 @@
         spread = jnp.dot(lines, taps_k, preferred_element_type=jnp.float32).astype(jnp.bfloat16)
         for slot in range(n_lon):
             met[slot, k * chunk : (k + 1) * chunk, :] = spread[slot * chunk : (slot + 1) * chunk]
-
-    for step in steps:
-        slot = n_lon - step
-        send_f(step).wait_recv()
-
-        @pl.when(has_up)
-        def _():
-            lat_f(0, slot).start()
-
-        @pl.when(has_down)
-        def _():
-            lat_f(1, slot).start()
-
-    for step in (1, n_lon - 1):
-        send_u(step).start()
 
     load_w.wait()
     for k in range(kernels):
@@ -386,7 +389,7 @@
             dma((groups,)), dma((groups,)), dma,
         ],
         compiler_params=pltpu.CompilerParams(
-            collective_id=0, has_side_effects=True, vmem_limit_bytes=56 * 1024 * 1024
+            collective_id=0, has_side_effects=True, vmem_limit_bytes=(20 + n_lon) * 1024 * 1024
         ),
         cost_estimate=pl.CostEstimate(
             flops=8_000_000_000, bytes_accessed=3_000_000, transcendentals=0

time: 30.5 us -> 36 us (1.18)
  local copies, waits for them, and re-layouts: 0 us -> 6.34 us
  Pallas kernels: 29 us -> 28 us
    unnamed x0 -> x16, local copies, waits for them, and re-layouts: none -> 6.34 us
    pallas_call x1, Pallas kernels: 27 us -> 26 us  [body(): pl.pallas_call(functools.partial(kernel, n_lat, n_lon), out_shape=(jax.Sh...]
where the time goes in v5:
time: 36 us; the launch traced here: 35.7 us
  Pallas kernels  28 us (78%)
  local copies, waits for them, and re-layouts  6.34 us (18%)
  between operations  1.31 us (4%)
    pallas_call x1, Pallas kernels, body(): pl.pallas_call(functools.partial(kernel, n_lat, n_lon), out_shape=(jax.Sh...  26 us
    unnamed x16, local copies, waits for them, and re-layouts  6.34 us
    pallas_call x1, Pallas kernels, body(): pl.pallas_call(finish, out_shape=tuple((jax.ShapeDtypeStruct(held.shape,...  2 us

profile of v5, /device:TPU:1, one launch (start us, length us, event | category | flops | bytes accessed | tf_op | source)
XLA Modules:
  0.0 35.7 jit_solution(879073986205955596)
XLA Ops:
  1.3 0.0 copy-start.3
  1.3 1.3 %copy-done.3 = bf16[9,256,256]{2,1,0:T(8,128)(2,1)S(1)} copy-done((bf16[9,256,256]{2,1,0:T(8,128)(2,1)S(1)}, bf16[9,256,256]{2,1,0:T(8,128)(2,1)}, u32[]{:S(2)}) %copy-start.3) | copy-done | bytes 1179672
  2.5 0.0 copy-start.4
  2.6 0.8 %copy-done.4 = bf16[256,1,128]{2,0,1:T(8,128)(2,1)S(1)} copy-done((bf16[256,1,128]{2,0,1:T(8,128)(2,1)S(1)}, bf16[256,1,128]{2,0,1:T(8,128)(2,1)}, u32[]{:S(2)}) %copy-start.4) | copy-done | bytes 65560
  3.4 0.0 copy-start.5
  3.4 0.8 %copy-done.5 = bf16[256,1,128]{2,0,1:T(8,128)(2,1)S(1)} copy-done((bf16[256,1,128]{2,0,1:T(8,128)(2,1)S(1)}, bf16[256,1,128]{2,0,1:T(8,128)(2,1)}, u32[]{:S(2)}) %copy-start.5) | copy-done | bytes 65560
  4.2 0.0 copy-start.6
  4.2 0.7 %copy-done.6 = bf16[1,9,3,2,64]{4,3,2,1,0:T(2,128)(2,1)S(1)} copy-done((bf16[1,9,3,2,64]{4,3,2,1,0:T(2,128)(2,1)S(1)}, bf16[1,9,3,2,64]{4,3,2,1,0:T(2,128)(2,1)}, u32[]{:S(2)}) %copy-start.6) | copy-done | bytes 6936
  4.9 0.0 copy-start.7
  4.9 0.7 %copy-done.7 = s32[1,2]{1,0:T(1,128)S(1)} copy-done((s32[1,2]{1,0:T(1,128)S(1)}, s32[1,2]{1,0:T(1,128)}, u32[]{:S(2)}) %copy-start.7) | copy-done | bytes 32
  5.6 26.0 %shard_map.85 = (bf16[256,128]{1,0:T(8,128)(2,1)S(1)}, bf16[256,128]{1,0:T(8,128)(2,1)S(1)}, f32[576,256]{1,0:T(8,128)S(1)}) custom-call(bf16[1,9,3,2,64]{4,3,2,1,0:T(2,128)(2,1)S(1)} %copy-done.6, s32[1]{0:T(128)S(6)} %copy.9.counts_ref, s32[1,2]{1,0:T(1,128)S(1)} %copy-done.7, bf16[256,128]{1,0:T(8,128)(2,1)S(1)} %bitcast.5, bf16[256,128]{1,0:T(8,128)(2,1)S(1)} %bitcast.6, ...), custom_call_target="tpu_custom_call" | custom-call | flops 8000000000 | bytes 3000000 | tf_op jit(solution)/shard_map/pallas_call | solution.py:360
  31.6 0.0 copy-start
  31.7 0.8 %copy-done = f32[576,256]{1,0:T(8,128)} copy-done((f32[576,256]{1,0:T(8,128)}, f32[576,256]{1,0:T(8,128)S(1)}, u32[]{:S(2)}) %copy-start) | copy-done | bytes 589848
  32.5 0.0 copy-start.1
  32.5 0.6 %copy-done.1 = bf16[256,128]{1,0:T(8,128)(2,1)} copy-done((bf16[256,128]{1,0:T(8,128)(2,1)}, bf16[256,128]{1,0:T(8,128)(2,1)S(1)}, u32[]{:S(2)}) %copy-start.1) | copy-done | bytes 65560
  33.1 0.0 copy-start.2
  33.1 0.6 %copy-done.2 = bf16[256,128]{1,0:T(8,128)(2,1)} copy-done((bf16[256,128]{1,0:T(8,128)(2,1)}, bf16[256,128]{1,0:T(8,128)(2,1)S(1)}, u32[]{:S(2)}) %copy-start.2) | copy-done | bytes 65560
  33.7 2.0 %shard_map.86 = (bf16[256,128]{1,0:T(8,128)(2,1)}, bf16[256,128]{1,0:T(8,128)(2,1)}, f32[576,256]{1,0:T(8,128)}) custom-call(bf16[256,128]{1,0:T(8,128)(2,1)} %copy-done.1, bf16[256,128]{1,0:T(8,128)(2,1)} %copy-done.2, f32[576,256]{1,0:T(8,128)} %copy-done), custom_call_target="tpu_custom_call" | custom-call | tf_op jit(solution)/shard_map/pallas_call | solution.py:401
Async XLA Ops:
  1.3 1.3 %copy-start.3 = (bf16[9,256,256]{2,1,0:T(8,128)(2,1)S(1)}, bf16[9,256,256]{2,1,0:T(8,128)(2,1)}, u32[]{:S(2)}) copy-start(bf16[9,256,256]{2,1,0:T(8,128)(2,1)} %w_hbm.1) | copy-start | bytes 3538948
  2.5 0.8 %copy-start.4 = (bf16[256,1,128]{2,0,1:T(8,128)(2,1)S(1)}, bf16[256,1,128]{2,0,1:T(8,128)(2,1)}, u32[]{:S(2)}) copy-start(bf16[256,1,128]{2,0,1:T(8,128)(2,1)} %param.6) | copy-start | bytes 196612
  3.4 0.8 %copy-start.5 = (bf16[256,1,128]{2,0,1:T(8,128)(2,1)S(1)}, bf16[256,1,128]{2,0,1:T(8,128)(2,1)}, u32[]{:S(2)}) copy-start(bf16[256,1,128]{2,0,1:T(8,128)(2,1)} %param.7) | copy-start | bytes 196612
  4.2 0.7 %copy-start.6 = (bf16[1,9,3,2,64]{4,3,2,1,0:T(2,128)(2,1)S(1)}, bf16[1,9,3,2,64]{4,3,2,1,0:T(2,128)(2,1)}, u32[]{:S(2)}) copy-start(bf16[1,9,3,2,64]{4,3,2,1,0:T(2,128)(2,1)} %taps_ref.1) | copy-start | bytes 20740
  4.9 0.7 %copy-start.7 = (s32[1,2]{1,0:T(1,128)S(1)}, s32[1,2]{1,0:T(1,128)}, u32[]{:S(2)}) copy-start(s32[1,2]{1,0:T(1,128)} %blocks_ref.1) | copy-start | bytes 28
  31.6 0.8 %copy-start = (f32[576,256]{1,0:T(8,128)}, f32[576,256]{1,0:T(8,128)S(1)}, u32[]{:S(2)}) copy-start(f32[576,256]{1,0:T(8,128)S(1)} %get-tuple-element.11.refs_2_) | copy-start | bytes 1769476
  32.5 0.6 %copy-start.1 = (bf16[256,128]{1,0:T(8,128)(2,1)}, bf16[256,128]{1,0:T(8,128)(2,1)S(1)}, u32[]{:S(2)}) copy-start(bf16[256,128]{1,0:T(8,128)(2,1)S(1)} %get-tuple-element.9.refs_0_) | copy-start | bytes 196612
  33.1 0.6 %copy-start.2 = (bf16[256,128]{1,0:T(8,128)(2,1)}, bf16[256,128]{1,0:T(8,128)(2,1)S(1)}, u32[]{:S(2)}) copy-start(bf16[256,128]{1,0:T(8,128)(2,1)S(1)} %get-tuple-element.10.refs_1_) | copy-start | bytes 196612

commit v6 on v5

--- a/solution.py
+++ b/solution.py
@@ -19,7 +19,7 @@
 
 def kernel(
     n_lat, n_lon, taps_ref, counts_ref, blocks_ref, f_ref, u_ref, w_hbm, out_ref, grad_ref, wg_ref,
-    w_ref, w_turned, f_mine, f_all, u_all, u_chunk, band, resp, met, rg, g_mine, g_got,
+    w_ref, w_turned, f_mine, f_all, u_all, u_chunk, band, resp, met, rg, g_mine, g_out, g_got,
     part, part_got, chip, result,
     zf_s, zf_r, zc_s, zc_r, zu_s, zu_r, lf_s, lf_r, g_s, g_r, p_s, p_r, x_s, x_r, q_s, q_r, w_s,
 ):
@@ -59,9 +59,25 @@
             device_id_type=MESH,
         )
 
-    def send_f(step):
-        slot = n_lon - step
-        return remote(f_mine, f_all.at[slot, 1], zf_s.at[step], zf_r.at[slot], lon_peer(step))
+    def hop_f(way, t):
+        slot = ((n_lon - (t - 1)) if way == 0 else (t - 1)) % n_lon
+        lands = n_lon - t if way == 0 else t
+        src = f_mine if t == 1 else f_all.at[slot, 1]
+        to = {"lat": a, "lon": b + 1 if way == 0 else b - 1}
+        return remote(src, f_all.at[lands, 1], zf_s.at[way, t], zf_r.at[lands], to)
+
+    def hops_out(way, t):
+        if way == 0:
+            return (b + 1 < n_lon) & (b - t + 1 >= 0)
+        return (b >= 1) & (b + t - 1 < n_lon)
+
+    def hops_in(way, t):
+        return b - t >= 0 if way == 0 else b + t < n_lon
+
+    def start_hop(way, t):
+        @pl.when(hops_out(way, t))
+        def _():
+            hop_f(way, t).start()
 
     def send_chunk(step):
         slot = n_lon - step
@@ -83,10 +99,10 @@
         )
 
     steps = sorted(range(1, n_lon), key=lambda step: min(step, n_lon - step))
+    for way in range(2):
+        start_hop(way, 1)
     for step in steps:
         send_chunk(step).start()
-    for step in steps:
-        send_f(step).start()
 
     @pl.when(has_up)
     def _():
@@ -130,20 +146,29 @@
     def _():
         f_all[:, 2] = jnp.zeros((n_lon, width, channels), f_all.dtype)
 
-    for step in steps:
-        slot = n_lon - step
-        send_f(step).wait_recv()
-
-        @pl.when(has_up)
-        def _():
-            lat_f(0, slot).start()
-
-        @pl.when(has_down)
-        def _():
-            lat_f(1, slot).start()
-
-    for step in (1, n_lon - 1):
-        send_u(step).start()
+    def pass_on(way, t):
+        slot = n_lon - t if way == 0 else t
+
+        @pl.when(hops_in(way, t))
+        def _():
+            hop_f(way, t).wait_recv()
+            if t + 1 < n_lon:
+                start_hop(way, t + 1)
+
+            @pl.when(has_up)
+            def _():
+                lat_f(0, slot).start()
+
+            @pl.when(has_down)
+            def _():
+                lat_f(1, slot).start()
+
+    for t in range(1, n_lon):
+        for way in range(2):
+            pass_on(way, t)
+        if t == 1:
+            for step in (1, n_lon - 1):
+                send_u(step).start()
 
     u_chunk[0] = u_ref[pl.ds(pl.multiple_of(b * chunk, chunk), chunk), :]
     for step in steps:
@@ -263,12 +288,13 @@
             rg[j], band[:, (2 - j) * 3 * width : (3 - j) * 3 * width],
             preferred_element_type=jnp.float32,
         )
-    for r in range(3):
-        g_mine[r] = terms[:, r * width : (r + 1) * width]
+    g_mine[...] = terms[:, width : 2 * width]
+    g_out[0] = terms[:, 2 * width :].astype(g_out.dtype)
+    g_out[1] = terms[:, :width].astype(g_out.dtype)
 
     def send_g(way):
         to = a + 1 if way == 0 else a - 1
-        return remote(g_mine.at[2 - 2 * way], g_got.at[way], g_s.at[way], g_r.at[way], lat_peer(to))
+        return remote(g_out.at[way], g_got.at[way], g_s.at[way], g_r.at[way], lat_peer(to))
 
     @pl.when(has_up)
     def _():
@@ -306,9 +332,9 @@
     def _():
         send_g(1).wait_recv()
 
-    below = jnp.where(has_down, g_got[0], 0.0)
-    above = jnp.where(has_up, g_got[1], 0.0)
-    grad_ref[...] = (g_mine[1] + below + above).astype(grad_ref.dtype)
+    below = jnp.where(has_down, g_got[0].astype(jnp.float32), 0.0)
+    above = jnp.where(has_up, g_got[1].astype(jnp.float32), 0.0)
+    grad_ref[...] = (g_mine[...] + below + above).astype(grad_ref.dtype)
 
     for g in range(groups):
         got_q(g).wait_recv()
@@ -317,8 +343,11 @@
         wg_ref[rows, channels // 2 :] = result[1, g]
 
     for step in range(1, n_lon):
-        send_f(step).wait_send()
         send_chunk(step).wait_send()
+        for way in range(2):
+            @pl.when(hops_out(way, step))
+            def _():
+                hop_f(way, step).wait_send()
     for step in (1, n_lon - 1):
         send_u(step).wait_send()
     for slot in range(n_lon):
@@ -377,19 +406,20 @@
             pltpu.VMEM((width, kernels * channels), bf16),
             pltpu.VMEM((n_lon, kernels * chunk, 3 * width), bf16),
             pltpu.VMEM((3, channels, kernels * width), bf16),
-            pltpu.VMEM((3, channels, width), f32),
-            pltpu.VMEM((2, channels, width), f32),
+            pltpu.VMEM((channels, width), f32),
+            pltpu.VMEM((2, channels, width), bf16),
+            pltpu.VMEM((2, channels, width), bf16),
             pltpu.VMEM((2, groups, rows, half), f32),
             pltpu.VMEM((groups, rows, half), f32),
             pltpu.VMEM((n_lat // 2, groups, rows, half), bf16),
             pltpu.VMEM((2, groups, rows, half), f32),
-            dma((n_lon,)), dma((n_lon,)), dma((n_lon,)), dma((n_lon,)), dma((n_lon,)), dma((n_lon,)),
+            dma((2, n_lon)), dma((n_lon,)), dma((n_lon,)), dma((n_lon,)), dma((n_lon,)), dma((n_lon,)),
             dma((2, n_lon)), dma((2, n_lon)), dma((2,)), dma((2,)),
             dma((groups,)), dma((groups,)), dma((groups, n_lat // 2)), dma((groups, n_lat // 2 + 1)),
             dma((groups,)), dma((groups,)), dma,
         ],
         compiler_params=pltpu.CompilerParams(
-            collective_id=0, has_side_effects=True, vmem_limit_bytes=(20 + n_lon) * 1024 * 1024
+            collective_id=0, has_side_effects=True, vmem_limit_bytes=56 * 1024 * 1024
         ),
         cost_estimate=pl.CostEstimate(
             flops=8_000_000_000, bytes_accessed=3_000_000, transcendentals=0

time: 36 us -> 33.5 us (0.931)
  local copies, waits for them, and re-layouts: 6.34 us -> 0 us
  Pallas kernels: 28 us -> 31.8 us
    unnamed x16 -> x0, local copies, waits for them, and re-layouts: 6.34 us -> none
    pallas_call x1, Pallas kernels: 26 us -> 29.8 us  [body(): pl.pallas_call(functools.partial(kernel, n_lat, n_lon), out_shape=(jax.Sh...]
where the time goes in v6:
time: 33.5 us; the launch traced here: 33.1 us
  Pallas kernels  31.8 us (95%)
  between operations  1.29 us (4%)
    pallas_call x1, Pallas kernels, body(): pl.pallas_call(functools.partial(kernel, n_lat, n_lon), out_shape=(jax.Sh...  29.8 us
    pallas_call x1, Pallas kernels, body(): pl.pallas_call(finish, out_shape=tuple((jax.ShapeDtypeStruct(held.shape,...  2.01 us

profile of v6, /device:TPU:1, one launch (start us, length us, event | category | flops | bytes accessed | tf_op | source)
XLA Modules:
  0.0 33.1 jit_solution(3248996576011991668)
XLA Ops:
  1.3 29.8 %shard_map.85 = (bf16[256,128]{1,0:T(8,128)(2,1)}, bf16[256,128]{1,0:T(8,128)(2,1)}, f32[576,256]{1,0:T(8,128)}) custom-call(bf16[1,9,3,2,64]{4,3,2,1,0:T(2,128)(2,1)} %taps_ref.1, s32[1]{0:T(128)S(6)} %copy.9.counts_ref, s32[1,2]{1,0:T(1,128)} %blocks_ref.1, bf16[256,128]{1,0:T(8,128)(2,1)} %bitcast.6, bf16[256,128]{1,0:T(8,128)(2,1)} %bitcast.7, ...), custom_call_target="tpu_custom_call" | custom-call | flops 8000000000 | bytes 3000000 | tf_op jit(solution)/shard_map/pallas_call | solution.py:389
  31.0 2.0 %shard_map.86 = (bf16[256,128]{1,0:T(8,128)(2,1)}, bf16[256,128]{1,0:T(8,128)(2,1)}, f32[576,256]{1,0:T(8,128)}) custom-call(bf16[256,128]{1,0:T(8,128)(2,1)} %get-tuple-element.9.refs_0_, bf16[256,128]{1,0:T(8,128)(2,1)} %get-tuple-element.10.refs_1_, f32[576,256]{1,0:T(8,128)} %get-tuple-element.11.refs_2_), custom_call_target="tpu_custom_call" | custom-call | tf_op jit(solution)/shard_map/pallas_call | solution.py:431

commit v7 on v5

--- a/solution.py
+++ b/solution.py
@@ -19,7 +19,7 @@
 
 def kernel(
     n_lat, n_lon, taps_ref, counts_ref, blocks_ref, f_ref, u_ref, w_hbm, out_ref, grad_ref, wg_ref,
-    w_ref, w_turned, f_mine, f_all, u_all, u_chunk, band, resp, met, rg, g_mine, g_got,
+    w_ref, w_turned, f_mine, f_all, u_all, u_chunk, band, resp, met, rg, g_mine, g_out, g_got,
     part, part_got, chip, result,
     zf_s, zf_r, zc_s, zc_r, zu_s, zu_r, lf_s, lf_r, g_s, g_r, p_s, p_r, x_s, x_r, q_s, q_r, w_s,
 ):
@@ -109,11 +109,8 @@
             tile = taps_ref[0, k, r].astype(jnp.float32)
             spread = jnp.concatenate([tile] * (2 * HALO // block_width) + [rest], axis=1)
             row = jnp.sum(jnp.where(used, spread, 0.0), axis=0, keepdims=True)
-            eight = pltpu.roll(
-                jnp.broadcast_to(row, (8, 4 * HALO)), 0, 1, stride=1, stride_axis=0
-            )
-            turned = jnp.concatenate(
-                [eight if p == 0 else pltpu.roll(eight, p, 1) for p in range(0, width, 8)], axis=0
+            turned = pltpu.roll(
+                jnp.broadcast_to(row, (width, 4 * HALO)), 0, 1, stride=1, stride_axis=0
             ).astype(jnp.bfloat16)
             for d in range(3):
                 band[k * width : (k + 1) * width, (3 * d + r) * width : (3 * d + r + 1) * width] = (
@@ -263,12 +260,13 @@
             rg[j], band[:, (2 - j) * 3 * width : (3 - j) * 3 * width],
             preferred_element_type=jnp.float32,
         )
-    for r in range(3):
-        g_mine[r] = terms[:, r * width : (r + 1) * width]
+    g_mine[...] = terms[:, width : 2 * width]
+    g_out[0] = terms[:, 2 * width :].astype(g_out.dtype)
+    g_out[1] = terms[:, :width].astype(g_out.dtype)
 
     def send_g(way):
         to = a + 1 if way == 0 else a - 1
-        return remote(g_mine.at[2 - 2 * way], g_got.at[way], g_s.at[way], g_r.at[way], lat_peer(to))
+        return remote(g_out.at[way], g_got.at[way], g_s.at[way], g_r.at[way], lat_peer(to))
 
     @pl.when(has_up)
     def _():
@@ -306,9 +304,9 @@
     def _():
         send_g(1).wait_recv()
 
-    below = jnp.where(has_down, g_got[0], 0.0)
-    above = jnp.where(has_up, g_got[1], 0.0)
-    grad_ref[...] = (g_mine[1] + below + above).astype(grad_ref.dtype)
+    below = jnp.where(has_down, g_got[0].astype(jnp.float32), 0.0)
+    above = jnp.where(has_up, g_got[1].astype(jnp.float32), 0.0)
+    grad_ref[...] = (g_mine[...] + below + above).astype(grad_ref.dtype)
 
     for g in range(groups):
         got_q(g).wait_recv()
@@ -377,8 +375,9 @@
             pltpu.VMEM((width, kernels * channels), bf16),
             pltpu.VMEM((n_lon, kernels * chunk, 3 * width), bf16),
             pltpu.VMEM((3, channels, kernels * width), bf16),
-            pltpu.VMEM((3, channels, width), f32),
-            pltpu.VMEM((2, channels, width), f32),
+            pltpu.VMEM((channels, width), f32),
+            pltpu.VMEM((2, channels, width), bf16),
+            pltpu.VMEM((2, channels, width), bf16),
             pltpu.VMEM((2, groups, rows, half), f32),
             pltpu.VMEM((groups, rows, half), f32),
             pltpu.VMEM((n_lat // 2, groups, rows, half), bf16),
@@ -389,7 +388,7 @@
             dma((groups,)), dma((groups,)), dma,
         ],
         compiler_params=pltpu.CompilerParams(
-            collective_id=0, has_side_effects=True, vmem_limit_bytes=(20 + n_lon) * 1024 * 1024
+            collective_id=0, has_side_effects=True, vmem_limit_bytes=56 * 1024 * 1024
         ),
         cost_estimate=pl.CostEstimate(
             flops=8_000_000_000, bytes_accessed=3_000_000, transcendentals=0

time: 36 us -> 29.9 us (0.83)
  local copies, waits for them, and re-layouts: 6.34 us -> 0 us
  Pallas kernels: 28 us -> 28.4 us
    unnamed x16 -> x0, local copies, waits for them, and re-layouts: 6.34 us -> none
where the time goes in v7:
time: 29.9 us; the launch traced here: 29.7 us
  Pallas kernels  28.4 us (95%)
  between operations  1.29 us (4%)
    pallas_call x1, Pallas kernels, body(): pl.pallas_call(functools.partial(kernel, n_lat, n_lon), out_shape=(jax.Sh...  26.4 us
    pallas_call x1, Pallas kernels, body(): pl.pallas_call(finish, out_shape=tuple((jax.ShapeDtypeStruct(held.shape,...  2.01 us

profile of v7, /device:TPU:1, one launch (start us, length us, event | category | flops | bytes accessed | tf_op | source)
XLA Modules:
  0.0 29.7 jit_solution(12007729593262448964)
XLA Ops:
  1.3 26.4 %shard_map.85 = (bf16[256,128]{1,0:T(8,128)(2,1)}, bf16[256,128]{1,0:T(8,128)(2,1)}, f32[576,256]{1,0:T(8,128)}) custom-call(bf16[1,9,3,2,64]{4,3,2,1,0:T(2,128)(2,1)} %taps_ref.1, s32[1]{0:T(128)S(6)} %copy.9.counts_ref, s32[1,2]{1,0:T(1,128)} %blocks_ref.1, bf16[256,128]{1,0:T(8,128)(2,1)} %bitcast.6, bf16[256,128]{1,0:T(8,128)(2,1)} %bitcast.7, ...), custom_call_target="tpu_custom_call" | custom-call | flops 8000000000 | bytes 3000000 | tf_op jit(solution)/shard_map/pallas_call | solution.py:358
  27.7 2.0 %shard_map.86 = (bf16[256,128]{1,0:T(8,128)(2,1)}, bf16[256,128]{1,0:T(8,128)(2,1)}, f32[576,256]{1,0:T(8,128)}) custom-call(bf16[256,128]{1,0:T(8,128)(2,1)} %get-tuple-element.9.refs_0_, bf16[256,128]{1,0:T(8,128)(2,1)} %get-tuple-element.10.refs_1_, f32[576,256]{1,0:T(8,128)} %get-tuple-element.11.refs_2_), custom_call_target="tpu_custom_call" | custom-call | tf_op jit(solution)/shard_map/pallas_call | solution.py:400

commit v8 on v7

--- a/solution.py
+++ b/solution.py
@@ -96,6 +96,18 @@
     def _():
         lat_f(1, 0).start()
 
+    def pass_on(step):
+        slot = n_lon - step
+        send_f(step).wait_recv()
+
+        @pl.when(has_up)
+        def _():
+            lat_f(0, slot).start()
+
+        @pl.when(has_down)
+        def _():
+            lat_f(1, slot).start()
+
     slots, block_width = taps_ref.shape[3:]
     lane = lax.broadcasted_iota(jnp.int32, (slots, 4 * HALO), 1)
     which = lax.broadcasted_iota(jnp.int32, (slots, 4 * HALO), 0)
@@ -105,6 +117,9 @@
     used = (which < counts_ref[0]) & (lane >= first) & (lane < first + block_width)
     rest = jnp.zeros((slots, 2 * HALO), jnp.float32)
     for k in range(kernels):
+        if k == 2 * kernels // 3:
+            for step in steps[:2]:
+                pass_on(step)
         for r in range(3):
             tile = taps_ref[0, k, r].astype(jnp.float32)
             spread = jnp.concatenate([tile] * (2 * HALO // block_width) + [rest], axis=1)
@@ -127,17 +142,8 @@
     def _():
         f_all[:, 2] = jnp.zeros((n_lon, width, channels), f_all.dtype)
 
-    for step in steps:
-        slot = n_lon - step
-        send_f(step).wait_recv()
-
-        @pl.when(has_up)
-        def _():
-            lat_f(0, slot).start()
-
-        @pl.when(has_down)
-        def _():
-            lat_f(1, slot).start()
+    for step in steps[2:]:
+        pass_on(step)
 
     for step in (1, n_lon - 1):
         send_u(step).start()

time: 29.9 us -> 29.8 us (level)
  no operation moved by 1% of the time
where the time goes in v8:
time: 29.8 us; the launch traced here: 29.5 us
  Pallas kernels  28.2 us (95%)
  between operations  1.29 us (4%)
    pallas_call x1, Pallas kernels, body(): pl.pallas_call(functools.partial(kernel, n_lat, n_lon), out_shape=(jax.Sh...  26.2 us
    pallas_call x1, Pallas kernels, body(): pl.pallas_call(finish, out_shape=tuple((jax.ShapeDtypeStruct(held.shape,...  2.01 us

profile of v8, /device:TPU:1, one launch (start us, length us, event | category | flops | bytes accessed | tf_op | source)
XLA Modules:
  0.0 29.5 jit_solution(5215290132228659345)
XLA Ops:
  1.3 26.2 %shard_map.85 = (bf16[256,128]{1,0:T(8,128)(2,1)}, bf16[256,128]{1,0:T(8,128)(2,1)}, f32[576,256]{1,0:T(8,128)}) custom-call(bf16[1,9,3,2,64]{4,3,2,1,0:T(2,128)(2,1)} %taps_ref.1, s32[1]{0:T(128)S(6)} %copy.9.counts_ref, s32[1,2]{1,0:T(1,128)} %blocks_ref.1, bf16[256,128]{1,0:T(8,128)(2,1)} %bitcast.6, bf16[256,128]{1,0:T(8,128)(2,1)} %bitcast.7, ...), custom_call_target="tpu_custom_call" | custom-call | flops 8000000000 | bytes 3000000 | tf_op jit(solution)/shard_map/pallas_call | solution.py:364
  27.5 2.0 %shard_map.86 = (bf16[256,128]{1,0:T(8,128)(2,1)}, bf16[256,128]{1,0:T(8,128)(2,1)}, f32[576,256]{1,0:T(8,128)}) custom-call(bf16[256,128]{1,0:T(8,128)(2,1)} %get-tuple-element.9.refs_0_, bf16[256,128]{1,0:T(8,128)(2,1)} %get-tuple-element.10.refs_1_, f32[576,256]{1,0:T(8,128)} %get-tuple-element.11.refs_2_), custom_call_target="tpu_custom_call" | custom-call | tf_op jit(solution)/shard_map/pallas_call | solution.py:406
